TPU v7x, 128 devices: a whole 4x4x4 slice. The times are simulated.
128 devices in a mesh: dp: 8 (over x, core), tp: 16 (over z, y).
Axes of the slice: x: 4, y: 4, z: 4, core: 2. Of those that a mesh axis runs over, the one named last changes fastest.
Arguments:
- queries: bfloat16 [512, 3, 64, 576], P('dp', None, 'tp'), may hold values from -16 to 16
- latent_cache: bfloat16 [512, 128, 576], P('dp'), may hold values from -6 to 6
- new_latent: bfloat16 [512, 3, 576], P('dp'), may hold values from -6 to 6
- lengths: int32 [512], P('dp'), may hold values from 1 to 128, 32768 in all
- value_up_weight: bfloat16 [64, 512, 128], P('tp'), may hold values from -0.25 to 0.25
- out_proj: bfloat16 [8192, 7168], P('tp'), may hold values from -0.0625 to 0.0625
- residual: bfloat16 [512, 3, 7168], P('dp'), may hold values from -150 to 150
- norm_gain: float32 [7168], replicated, may hold values from 0.5 to 1.5
- head_weight: bfloat16 [7168, 65536], P(None, ('dp', 'tp'))
- mask_bits: int32 [512, 3, 128], P(None, None, ('dp', 'tp')), may hold values from 0 to 65535
- targets: int32 [512, 3], replicated, may hold values from 0 to 65535
Outputs:
- log_probs: float32 [512, 3, 65536], P(('dp', 'tp'))
- entropy: float32 [512, 3], P(('dp', 'tp'))
- row_loss: float32 [512], P(('dp', 'tp'))
All inputs are finite; a program needn't handle non-finite values. No bound on the sum of `lengths` on one device may be relied on, other than what follows from the above.
Results may differ from a plain program's by a relative error of at most 0.02.
Values may be sent and summed in bfloat16 or wider, within the bound.
No kernel may reach another device: no remote copies, remote signals or barrier semaphores. Data moves between devices by JAX's collectives and lax.ppermute only.
A program may use at most 128 MiB of HBM per device.

v0:
```python
import jax
import jax.numpy as jnp
from jax import lax
from jax.sharding import PartitionSpec as P

LAT = 512


score_scale = 192.0 ** (-0.5)
neg_large = -1e30


def normalize(resid_rows, attn_rows, norm_gain):
    summed = resid_rows.astype(jnp.float32) + attn_rows
    mean_square = jnp.mean(summed * summed, axis=-1, keepdims=True)
    return (summed * lax.rsqrt(mean_square + 1e-06) * norm_gain).astype(jnp.bfloat16)


def body(
    queries,
    latent_cache,
    new_latent,
    lengths,
    value_up_weight,
    out_proj,
    residual,
    norm_gain,
    head_weight,
    mask_bits,
    targets,
):
    group_rows_count, steps_count = (queries.shape[0], queries.shape[1])
    context = latent_cache.shape[1]
    cache_scores = (
        jnp.einsum("rshk,rpk->rshp", queries, latent_cache, preferred_element_type=jnp.float32)
        * score_scale
    )
    new_scores = (
        jnp.einsum("rshk,rjk->rshj", queries, new_latent, preferred_element_type=jnp.float32)
        * score_scale
    )
    valid_cache = (lax.iota(jnp.int32, context)[None, :] < lengths[:, None])[:, None, None, :]
    position = lax.iota(jnp.int32, steps_count)
    valid_new = (position[None, :] <= position[:, None])[None, :, None, :]
    top_score = jnp.maximum(
        jnp.max(jnp.where(valid_cache, cache_scores, neg_large), axis=-1),
        jnp.max(jnp.where(valid_new, new_scores, neg_large), axis=-1),
    )[..., None]
    cache_exp = jnp.where(valid_cache, jnp.exp(cache_scores - top_score), 0.0)
    new_exp = jnp.where(valid_new, jnp.exp(new_scores - top_score), 0.0)
    denom = jnp.sum(cache_exp, axis=-1, keepdims=True) + jnp.sum(new_exp, axis=-1, keepdims=True)
    cache_probs = (cache_exp / denom).astype(jnp.bfloat16)
    new_probs = (new_exp / denom).astype(jnp.bfloat16)
    latent_result_rows = (
        jnp.einsum(
            "rshp,rpk->rshk",
            cache_probs,
            latent_cache[:, :, :LAT],
            preferred_element_type=jnp.float32,
        )
        + jnp.einsum(
            "rshj,rjk->rshk", new_probs, new_latent[:, :, :LAT], preferred_element_type=jnp.float32
        )
    ).astype(jnp.bfloat16)
    per_head_value_rows = jnp.einsum(
        "cezq,zql->cezl", latent_result_rows, value_up_weight, preferred_element_type=jnp.float32
    ).astype(jnp.bfloat16)
    per_head_value_rows = per_head_value_rows.reshape(group_rows_count, steps_count, -1)
    owned_row_block = group_rows_count // lax.axis_size("tp")
    attn_rows = lax.psum_scatter(
        jnp.dot(per_head_value_rows, out_proj, preferred_element_type=jnp.float32),
        "tp",
        scatter_dimension=0,
        tiled=True,
    )
    resid_rows = lax.dynamic_slice_in_dim(
        residual, lax.axis_index("tp") * owned_row_block, owned_row_block, 0
    )
    hidden = normalize(resid_rows, attn_rows, norm_gain)
    logits = jnp.dot(
        lax.all_gather(hidden, ("dp", "tp"), axis=0, tiled=True),
        head_weight,
        preferred_element_type=jnp.float32,
    )
    vocab_dev = head_weight.shape[1]
    devices_all = lax.axis_size("dp") * lax.axis_size("tp")
    device_id = lax.axis_index("dp") * lax.axis_size("tp") + lax.axis_index("tp")
    columns = lax.iota(jnp.int32, vocab_dev)
    tile_bit = columns // (vocab_dev // 16)
    bit_set = jnp.bitwise_and(jnp.right_shift(mask_bits, tile_bit[None, None, :]), 1) == 1
    local_target = targets - device_id * vocab_dev
    is_target = columns[None, None, :] == local_target[:, :, None]
    allowed = jnp.logical_or(bit_set, is_target)
    masked = jnp.where(allowed, logits, neg_large)
    target_part = jnp.sum(jnp.where(is_target, logits, 0.0), axis=-1)
    peak = lax.pmax(jnp.max(masked, axis=-1), ("dp", "tp"))
    shifted = logits - peak[..., None]
    weights = jnp.where(allowed, jnp.exp(shifted), 0.0)
    total, moment, target_logit = lax.psum(
        (jnp.sum(weights, axis=-1), jnp.sum(weights * shifted, axis=-1), target_part), ("dp", "tp")
    )
    log_partition_sum = peak + jnp.log(total)
    log_probs = jnp.where(allowed, logits - log_partition_sum[..., None], 0.0)
    entropy_all = jnp.log(total) - moment / total
    loss_all = jnp.mean(log_partition_sum - target_logit, axis=1)
    rows_per_device = logits.shape[0] // devices_all
    entropy = lax.dynamic_slice_in_dim(entropy_all, device_id * rows_per_device, rows_per_device, 0)
    row_loss = lax.dynamic_slice_in_dim(loss_all, device_id * rows_per_device, rows_per_device, 0)
    owned = lax.all_to_all(
        log_probs.astype(jnp.bfloat16), ("dp", "tp"), split_axis=0, concat_axis=2, tiled=True
    ).astype(log_probs.dtype)
    return (owned, entropy, row_loss)


def solution(mesh):
    placed = (
        P("dp", None, "tp", None),
        P("dp", None, None),
        P("dp", None, None),
        P("dp"),
        P("tp", None, None),
        P("tp", None),
        P("dp", None, None),
        P(),
        P(None, ("dp", "tp")),
        P(None, None, ("dp", "tp")),
        P(),
    )
    return jax.shard_map(
        body,
        mesh=mesh,
        in_specs=placed,
        out_specs=(P(("dp", "tp"), None, None), P(("dp", "tp"), None), P(("dp", "tp"))),
        check_vma=False,
    )
```

profile of v0, /device:TPU:0, one launch (start us, length us, event | category | flops | bytes accessed | tf_op | source)
XLA Modules:
  0.0 466.8 jit_solution(1983091131950708304)
XLA Ops:
  7.2 0.0 copy-start
  7.2 0.0 all-reduce.4.cloned.1.call-start
  7.2 0.8 iota_compare_fusion.1
  8.0 0.9 slice.7
  9.0 0.0 copy-done
  9.0 5.0 %fusion.18 = f32[64,3,4,3]{2,3,1,0:T(4,128)S(1)} fusion(bf16[64,3,4,576]{3,2,1,0:T(4,128)(2,1)S(1)} %copy-done, bf16[64,3,576,1]{2,0,1,3:T(8,128)(2,1)} %bitcast.53), kind=kOutput, calls=%fused_computation.32 | convolution fusion | flops 2654208 | bytes 1115136 | tf_op jit(solution)/shard_map/rshk,rjk->rshj/dot_general | solution.py:39
  14.0 0.2 copy.68
  14.2 0.1 select_reduce_fusion.3
  14.3 0.1 copy.69
  14.4 5.5 %select_reduce_fusion.2 = (f32[64,3,4]{2,1,0:T(4,128)S(1)}, f32[64,3,4,128]{3,2,1,0:T(4,128)S(1)}) fusion(pred[64,128]{1,0:T(8,128)(4,1)S(1)} %iota_compare_fusion.1, bf16[64,3,4,576]{3,2,1,0:T(4,128)(2,1)S(1)} %copy-done, bf16[64,128,576]{1,2,0:T(8,128)(2,1)} %param.12), kind=kOutput, calls=%fused_computation.27 | convolution fusion | flops 113540352 | bytes 10726400 | tf_op jit(solution)/shard_map/rshk,rpk->rshp/dot_general | solution.py:35
  20.0 0.1 copy.70
  20.1 0.1 fusion.27
  20.2 0.1 copy.71
  20.4 0.6 fusion.20
  21.0 0.1 copy.73
  21.1 5.7 %fusion.4 = f32[64,3,4,512]{3,2,1,0:T(4,128)S(1)} fusion(bf16[64,128,576]{1,2,0:T(8,128)(2,1)} %param.12, f32[64,3,4,128]{3,2,1,0:T(4,128)S(1)} %get-tuple-element.25, f32[64,3,4]{2,1,0:T(4,128)S(1)} %add.50, f32[64,3,4]{2,1,0:T(4,128)S(1)} %max.9, pred[64,128]{1,0:T(8,128)(4,1)S(1)} %iota_compare_fusion.1), kind=kOutput, calls=%fused_computation.4 | convolution fusion | flops 101056512 | bytes 10369024 | tf_op jit(solution)/shard_map/rshp,rpk->rshk/dot_general | solution.py:55
  26.8 0.1 divide_convert_fusion.2
  26.9 0.2 copy.75
  27.1 0.6 add_convert_fusion
  27.7 1.4 fusion.15
  29.2 7.1 %fusion.8 = f32[64,3,7168]{2,0,1:T(8,128)} fusion(bf16[512,7168]{1,0:T(8,128)(2,1)} %param.16, bf16[4,3,8,8,128]{4,3,2,1,0:T(8,128)(2,1)S(1)} %fusion.15), kind=kOutput, calls=%fused_computation.8 | convolution fusion | flops 1409286144 | bytes 13041664 | tf_op jit(solution)/shard_map/dot_general | solution.py:71
  36.3 0.0 all-reduce.4.cloned.1.call-update
  36.3 0.2 all-gather.2.cloned.1.call-start
  36.6 0.4 copy-done.5
  37.0 0.6 dynamic-slice
  38.2 116.0 %all-reduce.4.cloned.1.call-done = f32[64,3,7168]{2,0,1:T(8,128)} async-done(((f32[64,3,7168]{2,0,1:T(8,128)}), f32[64,3,7168]{2,0,1:T(8,128)}) %all-reduce.4.cloned.1.call-update) | async-done | bytes 5505040
  154.2 1.5 multiply_reduce_fusion.1
  155.7 0.0 copy-done.2
  155.7 1.4 multiply_convert_fusion
  157.1 0.8 copy.78
  157.9 0.0 all-gather.2.cloned.1.call-update
  157.9 0.0 copy-done.4
  158.0 0.0 copy-done.3
  158.0 99.7 %all-gather.2.cloned.1.call-done = bf16[512,3,7168]{2,1,0:T(4,128)(2,1)} async-done(((bf16[4,3,7168]{2,1,0:T(4,128)(2,1)}), bf16[512,3,7168]{2,1,0:T(4,128)(2,1)}) %all-gather.2.cloned.1.call-update) | async-done | bytes 22020112 | tf_op jit(solution)/shard_map/all_gather | solution.py:81
  257.7 22.5 %select_reduce_fusion.1 = (f32[512,3]{0,1:T(4,128)S(1)}, f32[512,3,512]{0,2,1:T(8,128)}) fusion(s32[512,3]{0,1:T(4,128)S(1)} %broadcast_subtract_fusion, s32[512]{0:T(512)S(1)} %add_select_fusion, s32[512,3]{0,1:T(4,128)S(1)} %bitcast.54, bf16[7168,512]{1,0:T(8,128)(2,1)} %param.19, bf16[512,3,7168]{2,1,0:T(4,128)(2,1)} %all-gather.2.cloned.1.call-done), kind=kOutput, calls=%fused_computation.15 | convolution fusion | flops 11279792128 | bytes 32526336 | tf_op jit(solution)/shard_map/dot_general | solution.py:80
  280.2 64.8 %pmax.7 = f32[512,3]{0,1:T(4,128)S(1)} all-reduce(f32[512,3]{0,1:T(4,128)S(1)} %get-tuple-element.26), channel_id=1, replica_groups=mesh['dp'=8,'tp'=16] {'dp','tp'}, use_global_device_ids=true, to_apply=%region_7.8 | all-reduce | flops 1536 | bytes 12288 | tf_op jit(solution)/shard_map/pmax | solution.py:96
  345.1 3.0 multiply_reduce_fusion
  348.1 64.6 %all-reduce.1 = (f32[512,3]{0,1:T(4,128)S(1)}, f32[512,3]{0,1:T(4,128)S(1)}, f32[512,3]{0,1:T(4,128)S(1)}) all-reduce(f32[512,3]{0,1:T(4,128)S(1)} %get-tuple-element.16, f32[512,3]{0,1:T(4,128)S(1)} %get-tuple-element.15, f32[512,3]{0,1:T(4,128)S(1)} %get-tuple-element.17), channel_id=1, replica_groups=mesh['dp'=8,'tp'=16] {'dp','tp'}, use_global_device_ids=true, to_apply=%region_9.10 | all-reduce | flops 4608 | bytes 36864 | tf_op jit(solution)/shard_map/psum | solution.py:99
  412.7 2.7 select_convert_fusion
  415.4 3.0 copy.81
  418.4 4.8 %all-to-all-start = ((bf16[512,3,512]{2,1,0:T(4,128)(2,1)}), bf16[512,3,512]{2,1,0:T(4,128)(2,1)S(1)}, u32[]{:S(2)}, u32[]{:S(2)}) async-start(bf16[512,3,512]{2,1,0:T(4,128)(2,1)} %copy.81), calls=%async_computation | async-start | bytes 4194304 | tf_op jit(solution)/shard_map/all_to_all | solution.py:109
  423.3 0.1 dynamic-slice_subtract_fusion
  423.3 0.7 copy.83
  424.0 0.6 dynamic_slice.11
  424.6 28.4 %all-to-all-done = bf16[512,3,512]{2,1,0:T(4,128)(2,1)S(1)} async-done(((bf16[512,3,512]{2,1,0:T(4,128)(2,1)}), bf16[512,3,512]{2,1,0:T(4,128)(2,1)S(1)}, u32[]{:S(2)}, u32[]{:S(2)}) %all-to-all-start) | async-done | bytes 1572896 | tf_op jit(solution)/shard_map/all_to_all | solution.py:109
  453.0 2.2 copy_convert_fusion
  455.1 4.8 %reshape.80 = f32[128,4,3,512]{3,1,0,2:T(4,128)} reshape(f32[512,3,512]{2,0,1:T(8,128)} %copy_convert_fusion) | data formatting | bytes 6291456 | tf_op jit(solution)/shard_map/convert_element_type | solution.py:111
  459.9 0.0 copy-done.1
  (14 shorter events, 0.1 us)
Async XLA Ops:
  7.2 1.8 copy-start
  7.2 147.0 %all-reduce.4.cloned.1.call-start = ((), (), s32[]{:S(2)}) async-start(), calls=%async_computation.2 | async-start | bytes 11010048
  36.3 0.7 copy-start.5
  36.3 119.4 %copy-start.2 = (f32[7168]{0:T(1024)S(1)}, f32[7168]{0:T(1024)}, u32[]{:S(2)}) copy-start(f32[7168]{0:T(1024)} %param.18) | copy-start | bytes 86020
  36.3 121.6 %copy-start.4 = (s32[512,3,1]{0,2,1:T(1,128)S(1)}, s32[512,3,1]{0,2,1:T(1,128)}, u32[]{:S(2)}) copy-start(s32[512,3,1]{0,2,1:T(1,128)} %param.20) | copy-start | bytes 18436
  36.3 121.7 %copy-start.3 = (s32[512,3]{0,1:T(4,128)S(1)}, s32[512,3]{0,1:T(4,128)}, u32[]{:S(2)}) copy-start(s32[512,3]{0,1:T(4,128)} %param.21) | copy-start | bytes 18436
  36.3 221.4 %all-gather.2.cloned.1.call-start = ((), (), s32[]{:S(2)}) async-start(), calls=%async_computation.1 | async-start | bytes 29589504 | tf_op jit(solution)/shard_map/all_gather | solution.py:81
  418.4 34.6 %all-to-all-start = ((bf16[512,3,512]{2,1,0:T(4,128)(2,1)}), bf16[512,3,512]{2,1,0:T(4,128)(2,1)S(1)}, u32[]{:S(2)}, u32[]{:S(2)}) async-start(bf16[512,3,512]{2,1,0:T(4,128)(2,1)} %copy.81), calls=%async_computation | async-start | bytes 4194304 | tf_op jit(solution)/shard_map/all_to_all | solution.py:109
  453.0 7.0 %copy-start.1 = (bf16[64,3,4,576]{3,2,1,0:T(4,128)(2,1)S(1)}, bf16[64,3,4,576]{3,2,1,0:T(4,128)(2,1)}, u32[]{:S(2)}) copy-start(bf16[64,3,4,576]{3,2,1,0:T(4,128)(2,1)} %param.11) | copy-start | bytes 2654212
Sparse Core Ops, SparseCore 0:
  36.5 117.7 all-reduce.3
  158.1 99.6 all-gather.1
where the time goes:
time: 468 us; the launch traced here: 467 us
  waiting for transfers between devices  244 us (52%)
  blocking collectives  129 us (28%)
  matrix products  48 us (10%)
  between operations  14.9 us (3%)
  other arithmetic  12.7 us (3%)
  local copies, waits for them, and re-layouts  12.6 us (3%)
  starting transfers between devices  5.1 us (1%)
    unnamed x3, waiting for transfers between devices  116 us
    all_gather x1, waiting for transfers between devices, body(): lax.all_gather(hidden, ('dp', 'tp'), axis=0, tiled=True)  99.7 us
    pmax x1, blocking collectives, body(): peak = lax.pmax(jnp.max(masked, axis=-1), ('dp', 'tp'))  64.8 us
    psum x1, blocking collectives, body(): lax.psum((jnp.sum(weights, axis=-1), jnp.sum(weights * shifted, axis=-1),...  64.6 us
    all_to_all x1, waiting for transfers between devices, body(): lax.all_to_all(log_probs.astype(jnp.bfloat16), ('dp', 'tp'), split_axis=0...  28.4 us
    dot_general x1, matrix products, body(): jnp.dot(lax.all_gather(hidden, ('dp', 'tp'), axis=0, tiled=True), head_we...  22.5 us
  transfers between devices with their start and end apart: 3, of which 3 were waited for; matrix products, arithmetic and copies ran while one was open for 0% of the time, Pallas kernels for 0%

commit v1 on v0

--- a/solution.py
+++ b/solution.py
@@ -16,19 +16,7 @@
     return (summed * lax.rsqrt(mean_square + 1e-06) * norm_gain).astype(jnp.bfloat16)
 
 
-def body(
-    queries,
-    latent_cache,
-    new_latent,
-    lengths,
-    value_up_weight,
-    out_proj,
-    residual,
-    norm_gain,
-    head_weight,
-    mask_bits,
-    targets,
-):
+def attention(queries, latent_cache, new_latent, lengths, value_up_weight):
     group_rows_count, steps_count = (queries.shape[0], queries.shape[1])
     context = latent_cache.shape[1]
     cache_scores = (
@@ -65,14 +53,31 @@
     per_head_value_rows = jnp.einsum(
         "cezq,zql->cezl", latent_result_rows, value_up_weight, preferred_element_type=jnp.float32
     ).astype(jnp.bfloat16)
-    per_head_value_rows = per_head_value_rows.reshape(group_rows_count, steps_count, -1)
-    owned_row_block = group_rows_count // lax.axis_size("tp")
-    attn_rows = lax.psum_scatter(
-        jnp.dot(per_head_value_rows, out_proj, preferred_element_type=jnp.float32),
-        "tp",
-        scatter_dimension=0,
-        tiled=True,
-    )
+    return per_head_value_rows.reshape(group_rows_count, steps_count, -1)
+
+
+def body(
+    queries,
+    latent_cache,
+    new_latent,
+    lengths,
+    value_up_weight,
+    out_proj,
+    residual,
+    norm_gain,
+    head_weight,
+    mask_bits,
+    targets,
+):
+    per_head_value_rows = attention(queries, latent_cache, new_latent, lengths, value_up_weight)
+    tp_count = lax.axis_size("tp")
+    owned_row_block = queries.shape[0] // tp_count
+    partial = jnp.dot(
+        per_head_value_rows, out_proj, preferred_element_type=jnp.float32
+    ).astype(jnp.bfloat16)
+    partial = partial.reshape((tp_count, owned_row_block) + partial.shape[1:])
+    partial = lax.all_to_all(partial, "tp", split_axis=0, concat_axis=0, tiled=True)
+    attn_rows = jnp.sum(partial.astype(jnp.float32), axis=0)
     resid_rows = lax.dynamic_slice_in_dim(
         residual, lax.axis_index("tp") * owned_row_block, owned_row_block, 0
     )
@@ -92,24 +97,40 @@
     is_target = columns[None, None, :] == local_target[:, :, None]
     allowed = jnp.logical_or(bit_set, is_target)
     masked = jnp.where(allowed, logits, neg_large)
-    target_part = jnp.sum(jnp.where(is_target, logits, 0.0), axis=-1)
-    peak = lax.pmax(jnp.max(masked, axis=-1), ("dp", "tp"))
-    shifted = logits - peak[..., None]
+    part_target = jnp.sum(jnp.where(is_target, logits, 0.0), axis=-1)
+    part_peak = jnp.max(masked, axis=-1)
+    shifted = logits - part_peak[..., None]
     weights = jnp.where(allowed, jnp.exp(shifted), 0.0)
-    total, moment, target_logit = lax.psum(
-        (jnp.sum(weights, axis=-1), jnp.sum(weights * shifted, axis=-1), target_part), ("dp", "tp")
-    )
+    part_total = jnp.sum(weights, axis=-1)
+    part_moment = jnp.sum(weights * shifted, axis=-1)
+    sent = jnp.where(allowed, shifted, 1.0).astype(jnp.bfloat16)
+    stats = jnp.stack([part_peak, part_total, part_moment, part_target], axis=0)
+    rows_per_device = logits.shape[0] // devices_all
+    steps = logits.shape[1]
+    stats = stats.reshape(4, devices_all, rows_per_device, steps).transpose(1, 0, 2, 3)
+    stats = lax.all_to_all(
+        stats.reshape(devices_all, -1), ("dp", "tp"), split_axis=0, concat_axis=0, tiled=True
+    ).reshape(devices_all, 4, rows_per_device, steps)
+    owned = lax.all_to_all(
+        sent.reshape(devices_all, rows_per_device, steps, vocab_dev),
+        ("dp", "tp"),
+        split_axis=0,
+        concat_axis=0,
+        tiled=True,
+    ).astype(jnp.float32)
+    peaks, totals, moments, target_parts = (stats[:, i] for i in range(4))
+    peak = jnp.max(peaks, axis=0)
+    lift = peaks - peak
+    scale = jnp.exp(lift)
+    total = jnp.sum(scale * totals, axis=0)
+    moment = jnp.sum(scale * (moments + lift * totals), axis=0)
+    target_logit = jnp.sum(target_parts, axis=0)
     log_partition_sum = peak + jnp.log(total)
-    log_probs = jnp.where(allowed, logits - log_partition_sum[..., None], 0.0)
-    entropy_all = jnp.log(total) - moment / total
-    loss_all = jnp.mean(log_partition_sum - target_logit, axis=1)
-    rows_per_device = logits.shape[0] // devices_all
-    entropy = lax.dynamic_slice_in_dim(entropy_all, device_id * rows_per_device, rows_per_device, 0)
-    row_loss = lax.dynamic_slice_in_dim(loss_all, device_id * rows_per_device, rows_per_device, 0)
-    owned = lax.all_to_all(
-        log_probs.astype(jnp.bfloat16), ("dp", "tp"), split_axis=0, concat_axis=2, tiled=True
-    ).astype(log_probs.dtype)
-    return (owned, entropy, row_loss)
+    log_probs = jnp.where(owned > 0.0, 0.0, owned + (peaks - log_partition_sum)[..., None])
+    log_probs = log_probs.transpose(1, 2, 0, 3).reshape(rows_per_device, steps, -1)
+    entropy = jnp.log(total) - moment / total
+    row_loss = jnp.mean(log_partition_sum - target_logit, axis=1)
+    return (log_probs, entropy, row_loss)
 
 
 def solution(mesh):

time: 468 us -> 295 us (0.63)
  blocking collectives: 129 us -> 0 us
  waiting for transfers between devices: 244 us -> 168 us
  starting transfers between devices: 5.1 us -> 20.9 us
  local copies, waits for them, and re-layouts: 12.6 us -> 21.1 us
  matrix products: 48 us -> 55 us
    unnamed x3 -> x1, waiting for transfers between devices: 116 us -> 0.02 us
    pmax x1 -> x0, blocking collectives: 64.8 us -> none  [body(): peak = lax.pmax(jnp.max(masked, axis=-1), ('dp', 'tp'))]
    psum x1 -> x0, blocking collectives: 64.6 us -> none  [body(): lax.psum((jnp.sum(weights, axis=-1), jnp.sum(weights * shifted, axis=-1),...]
    all_to_all x1 -> x3, waiting for transfers between devices: 28.4 us -> 69.6 us  [the longest x1 41.6 us: body(): lax.all_to_all(partial, 'tp', split_axis=0, concat_axis=0, tiled=True)]
    reshape x0 -> x6, local copies, waits for them, and re-layouts: none -> 16.3 us  [the longest x2 9.86 us: body(): partial = partial.reshape((tp_count, owned_row_block) + partial.shape[1:])]
    all_to_all x1 -> x3, starting transfers between devices: 4.84 us -> 20.9 us  [the longest x1 8.17 us: body(): lax.all_to_all(partial, 'tp', split_axis=0, concat_axis=0, tiled=True)]
    dot_general x1, matrix products: 22.5 us -> 30.5 us  [body(): jnp.dot(lax.all_gather(hidden, ('dp', 'tp'), axis=0, tiled=True), head_we...]
    convert_element_type x3 -> x1, local copies, waits for them, and re-layouts: 7.99 us -> 0.2 us  [attention(): new_probs = (new_exp / denom).astype(jnp.bfloat16)]
  transfers between devices with their start and end apart: 3 -> 4, of which waited for: 3 -> 4; matrix products, arithmetic and copies ran while one was open for 0% -> 2% of each run, Pallas kernels for 0% -> 0%
where the time goes in v1:
time: 295 us; the launch traced here: 294 us
  waiting for transfers between devices  168 us (57%)
  matrix products  55 us (19%)
  local copies, waits for them, and re-layouts  21.1 us (7%)
  starting transfers between devices  20.9 us (7%)
  other arithmetic  14.8 us (5%)
  between operations  14.3 us (5%)
    all_gather x1, waiting for transfers between devices, body(): lax.all_gather(hidden, ('dp', 'tp'), axis=0, tiled=True)  98.2 us
    all_to_all x1, waiting for transfers between devices, body(): lax.all_to_all(partial, 'tp', split_axis=0, concat_axis=0, tiled=True)  41.6 us
    dot_general x1, matrix products, body(): jnp.dot(lax.all_gather(hidden, ('dp', 'tp'), axis=0, tiled=True), head_we...  30.5 us
    all_to_all x1, waiting for transfers between devices, body(): lax.all_to_all(sent.reshape(devices_all, rows_per_device, steps, vocab_de...  22.6 us
    reshape x2, local copies, waits for them, and re-layouts, body(): partial = partial.reshape((tp_count, owned_row_block) + partial.shape[1:])  9.86 us
    all_to_all x1, starting transfers between devices, body(): lax.all_to_all(partial, 'tp', split_axis=0, concat_axis=0, tiled=True)  8.17 us
    all_to_all x1, starting transfers between devices, body(): lax.all_to_all(stats.reshape(devices_all, -1), ('dp', 'tp'), split_axis=0...  8.07 us
    dot_general x1, matrix products, body(): jnp.dot(per_head_value_rows, out_proj, preferred_element_type=jnp.float32)  6.23 us
  transfers between devices with their start and end apart: 4, of which 4 were waited for; matrix products, arithmetic and copies ran while one was open for 2% of the time, Pallas kernels for 0%

profile of v1, /device:TPU:0, one launch (start us, length us, event | category | flops | bytes accessed | tf_op | source)
XLA Modules:
  0.0 294.0 jit_solution(7929024452957381938)
XLA Ops:
  7.2 0.8 iota_compare_fusion.1
  8.0 0.9 slice.19
  9.0 5.0 %fusion.19 = f32[64,3,4,3]{2,3,1,0:T(4,128)S(1)} fusion(bf16[64,3,4,576]{3,2,1,0:T(4,128)(2,1)S(1)} %copy-done, bf16[64,3,576,1]{2,0,1,3:T(8,128)(2,1)} %bitcast.94), kind=kOutput, calls=%fused_computation.36 | convolution fusion | flops 2654208 | bytes 1115136 | tf_op jit(solution)/shard_map/rshk,rjk->rshj/dot_general | solution.py:27
  14.0 0.2 copy.124
  14.2 0.1 select_reduce_fusion.3
  14.3 0.1 copy.125
  14.4 5.5 %select_reduce_fusion.2 = (f32[64,3,4]{2,1,0:T(4,128)S(1)}, f32[64,3,4,128]{3,2,1,0:T(4,128)S(1)}) fusion(pred[64,128]{1,0:T(8,128)(4,1)S(1)} %iota_compare_fusion.1, bf16[64,3,4,576]{3,2,1,0:T(4,128)(2,1)S(1)} %copy-done, bf16[64,128,576]{1,2,0:T(8,128)(2,1)} %param.12), kind=kOutput, calls=%fused_computation.31 | convolution fusion | flops 113540352 | bytes 10726400 | tf_op jit(solution)/shard_map/rshk,rpk->rshp/dot_general | solution.py:23
  20.0 0.1 copy.126
  20.1 0.1 fusion.28
  20.2 0.1 copy.127
  20.3 0.6 fusion.21
  21.0 0.1 copy.129
  21.1 5.7 %fusion.4 = f32[64,3,4,512]{3,2,1,0:T(4,128)S(1)} fusion(bf16[64,128,576]{1,2,0:T(8,128)(2,1)} %param.12, f32[64,3,4,128]{3,2,1,0:T(4,128)S(1)} %get-tuple-element.15, f32[64,3,4]{2,1,0:T(4,128)S(1)} %add.53, f32[64,3,4]{2,1,0:T(4,128)S(1)} %max.7, pred[64,128]{1,0:T(8,128)(4,1)S(1)} %iota_compare_fusion.1), kind=kOutput, calls=%fused_computation.5 | convolution fusion | flops 101056512 | bytes 10369024 | tf_op jit(solution)/shard_map/rshp,rpk->rshk/dot_general | solution.py:43
  26.8 0.1 divide_convert_fusion.2
  26.9 0.2 copy.131
  27.1 0.6 add_convert_fusion
  27.7 1.4 fusion.16
  29.1 6.2 %convolution_convert_fusion = bf16[64,3,7168]{2,0,1:T(8,128)(2,1)} fusion(bf16[512,7168]{1,0:T(8,128)(2,1)} %param.16, bf16[4,3,8,8,128]{4,3,2,1,0:T(8,128)(2,1)S(1)} %fusion.16), kind=kOutput, calls=%fused_computation.4 | convolution fusion | flops 1410662400 | bytes 10289152 | tf_op jit(solution)/shard_map/dot_general | solution.py:75
  35.4 5.6 %reshape.112 = bf16[16,4,3,7168]{3,1,0,2:T(4,128)(2,1)} reshape(bf16[64,3,7168]{2,0,1:T(8,128)(2,1)} %convolution_convert_fusion) | data formatting | bytes 5505024 | tf_op jit(solution)/shard_map/reshape | solution.py:78
  41.0 4.3 %copy.134 = bf16[16,4,3,7168]{3,1,2,0:T(4,128)(2,1)} copy(bf16[16,4,3,7168]{3,1,0,2:T(4,128)(2,1)} %reshape.112) | data formatting | bytes 5505024 | tf_op jit(solution)/shard_map/reshape | solution.py:78
  45.2 8.2 %all-to-all-start = ((bf16[16,4,3,7168]{3,1,2,0:T(4,128)(2,1)}), bf16[16,4,3,7168]{3,1,2,0:T(4,128)(2,1)}, u32[]{:S(2)}, u32[]{:S(2)}) async-start(bf16[16,4,3,7168]{3,1,2,0:T(4,128)(2,1)} %copy.134), calls=%async_computation | async-start | bytes 5505024 | tf_op jit(solution)/shard_map/all_to_all | solution.py:79
  53.5 41.6 %all-to-all-done = bf16[16,4,3,7168]{3,1,2,0:T(4,128)(2,1)} async-done(((bf16[16,4,3,7168]{3,1,2,0:T(4,128)(2,1)}), bf16[16,4,3,7168]{3,1,2,0:T(4,128)(2,1)}, u32[]{:S(2)}, u32[]{:S(2)}) %all-to-all-start) | async-done | bytes 2752544 | tf_op jit(solution)/shard_map/all_to_all | solution.py:79
  95.1 3.0 %convert_reduce_fusion = f32[4,3,7168]{2,0,1:T(4,128)S(1)} fusion(bf16[16,4,3,7168]{3,1,2,0:T(4,128)(2,1)} %all-to-all-done), kind=kLoop, calls=%fused_computation.10 | loop fusion | flops 2666496 | bytes 3096576 | tf_op jit(solution)/shard_map/reduce_sum | solution.py:80
  98.1 1.2 multiply_reduce_fusion.1
  99.3 1.2 multiply_convert_fusion
  100.5 0.8 copy.135
  101.4 98.2 %all-gather.2.cloned.1.call-done = bf16[512,3,7168]{2,1,0:T(4,128)(2,1)} async-done(((bf16[4,3,7168]{2,1,0:T(4,128)(2,1)}), bf16[512,3,7168]{2,1,0:T(4,128)(2,1)}) %all-gather.2.cloned.1.call-update) | async-done | bytes 22020112 | tf_op jit(solution)/shard_map/all_gather | solution.py:86
  199.6 30.5 %select_reduce_fusion.1 = (f32[512,3]{0,1:T(4,128)S(1)}, f32[512,3,512]{2,0,1:T(8,128)}) fusion(s32[512,3]{0,1:T(4,128)S(1)} %broadcast_subtract_fusion, s32[512]{0:T(512)S(1)} %add_select_fusion, s32[512,3]{0,1:T(4,128)S(1)} %bitcast.95, bf16[7168,512]{1,0:T(8,128)(2,1)} %param.19, bf16[512,3,7168]{2,1,0:T(4,128)(2,1)} %all-gather.2.cloned.1.call-done), kind=kOutput, calls=%fused_computation.20 | convolution fusion | flops 11279792128 | bytes 32526336 | tf_op jit(solution)/shard_map/dot_general | solution.py:85
  230.1 0.2 stack.15
  230.3 5.0 %fusion.11 = (f32[512,3]{0,1:T(4,128)S(1)}, f32[512,3]{0,1:T(4,128)S(1)}, f32[512,3]{0,1:T(4,128)S(1)}, bf16[512,3,512]{2,0,1:T(8,128)(2,1)}) fusion(f32[512,3,512]{2,0,1:T(8,128)} %get-tuple-element.17, f32[512,3]{0,1:T(4,128)S(1)} %get-tuple-element.16, s32[512,3]{0,1:T(4,128)S(1)} %broadcast_subtract_fusion, s32[512]{0:T(512)S(1)} %add_select_fusion, ...), kind=kLoop, calls=%fused_computation.18 | loop fusion | flops 11005440 | bytes 4757504 | tf_op jit(solution)/shard_map/reduce_sum | solution.py:104
  235.3 0.2 stack.16
  235.6 0.1 copy.138
  235.7 0.2 stack.17
  236.0 0.2 stack.18
  236.4 0.7 copy.143
  237.1 8.1 %all-to-all-start.2 = ((f32[128,1,48]{2,1,0:T(1,128)}), f32[128,1,48]{2,1,0:T(1,128)S(1)}, u32[]{:S(2)}, u32[]{:S(2)}) async-start(f32[128,1,48]{2,1,0:T(1,128)} %copy.143), calls=%async_computation.2 | async-start | bytes 131072 | tf_op jit(solution)/shard_map/all_to_all | solution.py:111
  245.2 2.4 reshape.113
  247.6 1.7 copy.137
  249.2 5.4 %all-to-all-done.2 = f32[128,1,48]{2,1,0:T(1,128)S(1)} async-done(((f32[128,1,48]{2,1,0:T(1,128)}), f32[128,1,48]{2,1,0:T(1,128)S(1)}, u32[]{:S(2)}, u32[]{:S(2)}) %all-to-all-start.2) | async-done | bytes 24608 | tf_op jit(solution)/shard_map/all_to_all | solution.py:111
  254.7 4.6 %all-to-all-start.1 = ((bf16[128,4,3,512]{3,1,2,0:T(4,128)(2,1)}), bf16[128,4,3,512]{3,1,2,0:T(4,128)(2,1)S(1)}, u32[]{:S(2)}, u32[]{:S(2)}) async-start(bf16[128,4,3,512]{3,1,2,0:T(4,128)(2,1)} %copy.137), calls=%async_computation.1 | async-start | bytes 3145728 | tf_op jit(solution)/shard_map/all_to_all | solution.py:114
  259.4 0.1 slice_reduce_fusion
  259.5 0.2 fusion.31
  259.7 0.7 subtract_reduce_fusion
  260.4 0.2 copy.145
  260.6 0.5 broadcast_multiply_fusion
  261.1 22.6 %all-to-all-done.1 = bf16[128,4,3,512]{3,1,2,0:T(4,128)(2,1)S(1)} async-done(((bf16[128,4,3,512]{3,1,2,0:T(4,128)(2,1)}), bf16[128,4,3,512]{3,1,2,0:T(4,128)(2,1)S(1)}, u32[]{:S(2)}, u32[]{:S(2)}) %all-to-all-start.1) | async-done | bytes 1572896 | tf_op jit(solution)/shard_map/all_to_all | solution.py:114
  283.7 1.1 fusion.10
  284.8 2.3 copy.158
  (28 shorter events, 0.7 us)
Async XLA Ops:
  7.2 1.8 copy-start
  45.2 49.9 %all-to-all-start = ((bf16[16,4,3,7168]{3,1,2,0:T(4,128)(2,1)}), bf16[16,4,3,7168]{3,1,2,0:T(4,128)(2,1)}, u32[]{:S(2)}, u32[]{:S(2)}) async-start(bf16[16,4,3,7168]{3,1,2,0:T(4,128)(2,1)} %copy.134), calls=%async_computation | async-start | bytes 5505024 | tf_op jit(solution)/shard_map/all_to_all | solution.py:79
  53.4 45.9 %copy-start.2 = (f32[7168]{0:T(1024)S(1)}, f32[7168]{0:T(1024)}, u32[]{:S(2)}) copy-start(f32[7168]{0:T(1024)} %param.18) | copy-start | bytes 86020
  53.4 47.9 %copy-start.4 = (s32[512,3,1]{0,2,1:T(1,128)S(1)}, s32[512,3,1]{0,2,1:T(1,128)}, u32[]{:S(2)}) copy-start(s32[512,3,1]{0,2,1:T(1,128)} %param.20) | copy-start | bytes 18436
  53.4 47.9 %copy-start.3 = (s32[512,3]{0,1:T(4,128)S(1)}, s32[512,3]{0,1:T(4,128)}, u32[]{:S(2)}) copy-start(s32[512,3]{0,1:T(4,128)} %param.21) | copy-start | bytes 18436
  53.4 146.2 %all-gather.2.cloned.1.call-start = ((), (), s32[]{:S(2)}) async-start(), calls=%async_computation.3 | async-start | bytes 29589504 | tf_op jit(solution)/shard_map/all_gather | solution.py:86
  237.1 17.5 %all-to-all-start.2 = ((f32[128,1,48]{2,1,0:T(1,128)}), f32[128,1,48]{2,1,0:T(1,128)S(1)}, u32[]{:S(2)}, u32[]{:S(2)}) async-start(f32[128,1,48]{2,1,0:T(1,128)} %copy.143), calls=%async_computation.2 | async-start | bytes 131072 | tf_op jit(solution)/shard_map/all_to_all | solution.py:111
  254.7 29.1 %all-to-all-start.1 = ((bf16[128,4,3,512]{3,1,2,0:T(4,128)(2,1)}), bf16[128,4,3,512]{3,1,2,0:T(4,128)(2,1)S(1)}, u32[]{:S(2)}, u32[]{:S(2)}) async-start(bf16[128,4,3,512]{3,1,2,0:T(4,128)(2,1)} %copy.137), calls=%async_computation.1 | async-start | bytes 3145728 | tf_op jit(solution)/shard_map/all_to_all | solution.py:114
  283.7 3.4 %copy-start.1 = (bf16[64,3,4,576]{3,2,1,0:T(4,128)(2,1)S(1)}, bf16[64,3,4,576]{3,2,1,0:T(4,128)(2,1)}, u32[]{:S(2)}) copy-start(bf16[64,3,4,576]{3,2,1,0:T(4,128)(2,1)} %param.11) | copy-start | bytes 2654212
Sparse Core Ops, SparseCore 0:
  101.4 98.1 all-gather.1

commit v2 on v1

v2 whole, which is shorter than its diff:
```python
import jax
import jax.numpy as jnp
from jax import lax
from jax.sharding import PartitionSpec as P

LAT = 512
TP = ("z", "y")
SAME = ("x", "z", "y")


score_scale = 192.0 ** (-0.5)
neg_large = -1e30


def attention(queries, latent_cache, new_latent, lengths, value_up_weight):
    group_rows_count, steps_count = (queries.shape[0], queries.shape[1])
    context = latent_cache.shape[1]
    cache_scores = (
        jnp.einsum("rshk,rpk->rshp", queries, latent_cache, preferred_element_type=jnp.float32)
        * score_scale
    )
    new_scores = (
        jnp.einsum("rshk,rjk->rshj", queries, new_latent, preferred_element_type=jnp.float32)
        * score_scale
    )
    valid_cache = (lax.iota(jnp.int32, context)[None, :] < lengths[:, None])[:, None, None, :]
    position = lax.iota(jnp.int32, steps_count)
    valid_new = (position[None, :] <= position[:, None])[None, :, None, :]
    top_score = jnp.maximum(
        jnp.max(jnp.where(valid_cache, cache_scores, neg_large), axis=-1),
        jnp.max(jnp.where(valid_new, new_scores, neg_large), axis=-1),
    )[..., None]
    cache_exp = jnp.where(valid_cache, jnp.exp(cache_scores - top_score), 0.0)
    new_exp = jnp.where(valid_new, jnp.exp(new_scores - top_score), 0.0)
    denom = jnp.sum(cache_exp, axis=-1, keepdims=True) + jnp.sum(new_exp, axis=-1, keepdims=True)
    cache_probs = (cache_exp / denom).astype(jnp.bfloat16)
    new_probs = (new_exp / denom).astype(jnp.bfloat16)
    latent_result_rows = (
        jnp.einsum(
            "rshp,rpk->rshk",
            cache_probs,
            latent_cache[:, :, :LAT],
            preferred_element_type=jnp.float32,
        )
        + jnp.einsum(
            "rshj,rjk->rshk", new_probs, new_latent[:, :, :LAT], preferred_element_type=jnp.float32
        )
    ).astype(jnp.bfloat16)
    per_head_value_rows = jnp.einsum(
        "cezq,zql->cezl", latent_result_rows, value_up_weight, preferred_element_type=jnp.float32
    ).astype(jnp.bfloat16)
    return per_head_value_rows.reshape(group_rows_count, steps_count, -1)


def body(
    queries,
    latent_cache,
    new_latent,
    lengths,
    value_up_weight,
    out_proj,
    residual,
    norm_gain,
    head_weight,
    mask_bits,
    targets,
):
    rows, steps = queries.shape[:2]
    width = residual.shape[2]
    half = width // 2
    vocab_dev = head_weight.shape[1]
    x_count, cores, tp_count = lax.axis_size("x"), lax.axis_size("core"), lax.axis_size(TP)
    core, tp = lax.axis_index("core"), lax.axis_index(TP)
    groups = tp_count // 2
    group_rows = rows // groups
    pairs = steps * group_rows
    weights_pair = lax.all_gather(head_weight, "core", axis=0)

    def of_core(full, which):
        cut = full.reshape(x_count, cores, groups, group_rows, steps)
        cut = lax.dynamic_index_in_dim(cut, which, 1, keepdims=False)
        return cut.transpose(0, 1, 3, 2).reshape(-1)

    words_own = of_core(mask_bits, core)
    words_other = lax.ppermute(of_core(mask_bits, 1 - core), "core", ((0, 1), (1, 0)))
    words = jnp.where(core == 0, jnp.stack([words_own, words_other]), jnp.stack([words_other, words_own]))
    row_targets = of_core(targets, core)

    values = attention(queries, latent_cache, new_latent, lengths, value_up_weight)
    values = values.reshape(groups, group_rows, steps, -1).transpose(0, 2, 1, 3)
    values = values.reshape(groups * pairs, -1)
    partial = jnp.stack(
        [
            jnp.dot(values, out_proj[:, :half], preferred_element_type=jnp.float32),
            jnp.dot(values, out_proj[:, half:], preferred_element_type=jnp.float32),
        ]
    ).astype(jnp.bfloat16)
    partial = lax.all_to_all(
        partial.reshape(tp_count, pairs, half), TP, split_axis=0, concat_axis=0, tiled=True
    )
    partial, weights_pair = lax.optimization_barrier((partial, weights_pair))
    own_half, own_group = tp // groups, tp % groups
    resid = lax.dynamic_slice(
        residual.transpose(1, 0, 2),
        (0, own_group * group_rows, own_half * half),
        (steps, group_rows, half),
    ).reshape(pairs, half)
    gain = lax.dynamic_slice_in_dim(norm_gain, own_half * half, half, 0)
    summed = resid.astype(jnp.float32) + jnp.sum(partial.astype(jnp.float32), axis=0)
    squares = jnp.sum(summed * summed, axis=-1)
    hidden = (summed * gain).astype(jnp.bfloat16)
    hidden = lax.all_gather(hidden, SAME, axis=0).reshape(x_count, 2, groups * pairs, half)
    squares = lax.all_gather(squares, SAME, axis=0).reshape(x_count, 2, groups * pairs)
    norm = lax.rsqrt(jnp.sum(squares, axis=1) / width + 1e-06).reshape(-1)

    columns = lax.iota(jnp.int32, vocab_dev)
    tile_bit = columns // (vocab_dev // 16)
    shifted_by_core, allowed_by_core, target_parts, masked_peaks = [], [], [], []
    for which in range(cores):
        weight = weights_pair[which]
        logits = jnp.dot(
            hidden[:, 0].reshape(-1, half), weight[:half], preferred_element_type=jnp.float32
        ) + jnp.dot(
            hidden[:, 1].reshape(-1, half), weight[half:], preferred_element_type=jnp.float32
        )
        logits = logits * norm[:, None]
        shard = (lax.axis_index("x") * cores + which) * tp_count + tp
        bit_set = jnp.bitwise_and(jnp.right_shift(words[which][:, None], tile_bit[None, :]), 1) == 1
        is_target = columns[None, :] == (row_targets - shard * vocab_dev)[:, None]
        allowed = jnp.logical_or(bit_set, is_target)
        shifted_by_core.append(logits)
        allowed_by_core.append(allowed)
        target_parts.append(jnp.sum(jnp.where(is_target, logits, 0.0), axis=-1))
        masked_peaks.append(jnp.max(jnp.where(allowed, logits, neg_large), axis=-1))
    part_peak = jnp.maximum(*masked_peaks)
    part_total, part_moment, sent = 0.0, 0.0, []
    for which in range(cores):
        shifted = shifted_by_core[which] - part_peak[:, None]
        weight = jnp.where(allowed_by_core[which], jnp.exp(shifted), 0.0)
        part_total = part_total + jnp.sum(weight, axis=-1)
        part_moment = part_moment + jnp.sum(weight * shifted, axis=-1)
        sent.append(jnp.where(allowed_by_core[which], shifted, 1.0).astype(jnp.bfloat16))
    stats = jnp.stack([part_peak, part_total, part_moment, target_parts[0] + target_parts[1]])
    stats = lax.all_gather(stats, SAME, axis=0)
    own_rows = rows // tp_count
    spread = (x_count, groups, steps, group_rows // own_rows, own_rows)
    sent = jnp.stack([one.reshape(spread + (vocab_dev,)) for one in sent], axis=4)
    sent = sent.transpose(0, 1, 3, 2, 4, 5, 6)
    sent = sent.reshape(x_count * tp_count, steps * cores * own_rows, vocab_dev)
    owned = lax.all_to_all(sent, SAME, split_axis=0, concat_axis=0, tiled=True)
    owned = owned.reshape(x_count, tp_count, steps, cores, own_rows, vocab_dev)

    stats = lax.dynamic_slice(
        stats.reshape((x_count * tp_count, 4) + spread),
        (0, 0, lax.axis_index("x"), tp // 2, 0, tp % 2, 0),
        (x_count * tp_count, 4, 1, 1, steps, 1, own_rows),
    ).reshape(x_count, tp_count, 4, steps, own_rows)
    peaks, totals, moments, target_part = (stats[:, :, i] for i in range(4))
    peak = jnp.max(peaks, axis=(0, 1))
    lift = peaks - peak
    scale = jnp.exp(lift)
    total = jnp.sum(scale * totals, axis=(0, 1))
    moment = jnp.sum(scale * (moments + lift * totals), axis=(0, 1))
    target_logit = jnp.sum(target_part, axis=(0, 1))
    log_partition_sum = peak + jnp.log(total)
    offset = (peaks - log_partition_sum)[:, :, :, None, :, None]
    owned = owned.astype(jnp.float32)
    log_probs = jnp.where(owned > 0.0, 0.0, owned + offset)
    log_probs = log_probs.transpose(4, 2, 0, 3, 1, 5).reshape(own_rows, steps, -1)
    entropy = (jnp.log(total) - moment / total).T
    row_loss = jnp.mean(log_partition_sum - target_logit, axis=0)
    return (log_probs, entropy, row_loss)


def solution(mesh):
    mesh = jax.sharding.Mesh(mesh.devices.reshape(4, 2, 4, 4), ("x", "core", "z", "y"))
    dp, all_axes = ("x", "core"), ("x", "core", "z", "y")
    placed = (
        P(dp, None, TP, None),
        P(dp, None, None),
        P(dp, None, None),
        P(dp),
        P(TP, None, None),
        P(TP, None),
        P(dp, None, None),
        P(),
        P(None, all_axes),
        P(None, None, all_axes),
        P(),
    )
    return jax.shard_map(
        body,
        mesh=mesh,
        in_specs=placed,
        out_specs=(P(all_axes, None, None), P(all_axes, None), P(all_axes)),
        check_vma=False,
    )
```

time: 295 us -> 511 us (1.73)
  blocking collectives: 0 us -> 354 us
  waiting for transfers between devices: 168 us -> 42.6 us
  matrix products: 55 us -> 43.9 us
  starting transfers between devices: 20.9 us -> 13 us
  local copies, waits for them, and re-layouts: 21.1 us -> 27.3 us
    all_gather x0 -> x2, blocking collectives: none -> 354 us  [the longest x1 182 us: body(): stats = lax.all_gather(stats, SAME, axis=0)]
    all_gather x1 -> x2, waiting for transfers between devices: 98.2 us -> 0.01 us  [the longest x1 0.01 us: body(): weights_pair = lax.all_gather(head_weight, 'core', axis=0)]
    all_to_all x3 -> x2, waiting for transfers between devices: 69.6 us -> 41.2 us  [the longest x1 41.2 us: body(): lax.all_to_all(partial.reshape(tp_count, pairs, half), TP, split_axis=0,...]
    dot_general x2 -> x6, matrix products: 36.7 us -> 25.6 us  [the longest x2 12.1 us: body(): jnp.dot(hidden[:, 1].reshape(-1, half), weight[half:], preferred_element_...]
    slice x0 -> x2, local copies, waits for them, and re-layouts: none -> 9.01 us  [the longest x1 8.98 us: body(): hidden[:, 0].reshape(-1, half)]
    reshape x6 -> x7, local copies, waits for them, and re-layouts: 16.3 us -> 7.67 us  [the longest x1 5.31 us: body(): log_probs.transpose(4, 2, 0, 3, 1, 5).reshape(own_rows, steps, -1)]
    all_to_all x3 -> x2, starting transfers between devices: 20.9 us -> 12.9 us  [the longest x1 8.21 us: body(): lax.all_to_all(partial.reshape(tp_count, pairs, half), TP, split_axis=0,...]
  transfers between devices with their start and end apart: 4 -> 5, of which waited for: 4 -> 2; matrix products, arithmetic and copies ran while one was open for 2% -> 7% of each run, Pallas kernels for 0% -> 0%
where the time goes in v2:
time: 511 us; the launch traced here: 510 us
  blocking collectives  354 us (69%)
  matrix products  43.9 us (9%)
  waiting for transfers between devices  42.6 us (8%)
  local copies, waits for them, and re-layouts  27.3 us (5%)
  other arithmetic  14.8 us (3%)
  between operations  14.6 us (3%)
  starting transfers between devices  13 us (3%)
    all_gather x1, blocking collectives, body(): stats = lax.all_gather(stats, SAME, axis=0)  182 us
    all_gather x1, blocking collectives, body(): lax.all_gather(squares, SAME, axis=0).reshape(x_count, 2, groups * pairs)  171 us
    all_to_all x1, waiting for transfers between devices, body(): lax.all_to_all(partial.reshape(tp_count, pairs, half), TP, split_axis=0,...  41.2 us
    dot_general x2, matrix products, body(): jnp.dot(hidden[:, 1].reshape(-1, half), weight[half:], preferred_element_...  12.1 us
  transfers between devices with their start and end apart: 5, of which 2 were waited for; matrix products, arithmetic and copies ran while one was open for 7% of the time, Pallas kernels for 0%

profile of v2, /device:TPU:0, one launch (start us, length us, event | category | flops | bytes accessed | tf_op | source)
XLA Modules:
  0.0 510.3 jit_solution(4362847940971907761)
XLA Ops:
  7.2 0.7 all-gather.9.cloned.1.call-update
  7.9 0.3 copy-done.3
  8.2 0.3 copy-done
  8.5 4.1 fusion.41
  12.6 0.2 copy.103
  12.9 0.1 copy.104
  13.1 5.5 %select_reduce_fusion.4 = (f32[64,3,4]{2,1,0:T(4,128)S(1)}, f32[64,3,4,128]{3,2,1,0:T(4,128)S(1)}) fusion(pred[64,128]{1,0:T(8,128)(4,1)S(1)} %iota_compare_fusion.2, bf16[64,3,4,576]{3,2,1,0:T(4,128)(2,1)S(1)} %copy-done, bf16[64,128,576]{1,2,0:T(8,128)(2,1)} %param.12), kind=kOutput, calls=%fused_computation.57 | convolution fusion | flops 113540352 | bytes 10726400 | tf_op jit(solution)/shard_map/rshk,rpk->rshp/dot_general | solution.py:19
  19.0 0.6 fusion.43
  19.8 0.2 copy.110
  20.0 7.7 %fusion.2 = f32[64,3,4,512]{3,2,1,0:T(4,128)S(1)} fusion(bf16[64,128,576]{1,2,0:T(8,128)(2,1)} %param.12, f32[64,3,4,128]{3,2,1,0:T(4,128)S(1)} %get-tuple-element.48, f32[64,3,4]{2,1,0:T(4,128)S(1)} %add.156, f32[64,3,4]{2,1,0:T(4,128)S(1)} %max.24, pred[64,128]{1,0:T(8,128)(4,1)S(1)} %iota_compare_fusion.2), kind=kOutput, calls=%fused_computation.2 | convolution fusion | flops 101056512 | bytes 10369024 | tf_op jit(solution)/shard_map/rshp,rpk->rshk/dot_general | solution.py:39
  27.8 0.6 add_convert_fusion
  28.4 0.6 copy-done.8
  29.0 0.4 fusion.32
  29.4 0.2 copy.112
  29.7 3.6 fusion.6
  33.3 3.4 fusion.5
  36.8 1.8 pad_maximum_fusion
  38.5 8.2 %all-to-all-start = ((bf16[16,24,3584]{2,1,0:T(8,128)(2,1)}), bf16[16,24,3584]{2,1,0:T(8,128)(2,1)}, u32[]{:S(2)}, u32[]{:S(2)}) async-start(bf16[16,24,3584]{2,1,0:T(8,128)(2,1)} %bitcast.154), calls=%async_computation | async-start | bytes 5505024 | tf_op jit(solution)/shard_map/all_to_all | solution.py:98
  46.9 41.2 %all-to-all-done = bf16[16,24,3584]{2,1,0:T(8,128)(2,1)} async-done(((bf16[16,24,3584]{2,1,0:T(8,128)(2,1)}), bf16[16,24,3584]{2,1,0:T(8,128)(2,1)}, u32[]{:S(2)}, u32[]{:S(2)}) %all-to-all-start) | async-done | bytes 2752544 | tf_op jit(solution)/shard_map/all_to_all | solution.py:98
  88.1 2.2 convert_reduce_fusion
  90.3 1.6 fusion.40
  92.9 0.7 collective-permute-done
  93.7 1.1 fusion.37
  94.9 171.5 %all-gather.2 = f32[64,1,24]{2,1,0:T(1,128)S(1)} all-gather(f32[1,1,24]{2,1,0:T(1,128)S(1)} %reshape.264), channel_id=1, replica_groups=mesh['x'=4,'core'=2,'z'=4,'y'=4] {'x','z','y'}, dimensions={0}, use_global_device_ids=true | all-gather | bytes 6240 | tf_op jit(solution)/shard_map/all_gather | solution.py:113
  266.4 0.5 broadcast.146
  266.9 0.7 reduce.11
  267.8 9.0 %fusion.59 = (bf16[4,1,192,3584]{3,2,1,0:T(8,128)(2,1)}, bf16[4,1,192,3584]{3,2,1,0:T(8,128)(2,1)}) fusion(bf16[4,2,192,3584]{3,2,1,0:T(8,128)(2,1)} %bitcast.153), kind=kLoop, calls=%fused_computation.117 | loop fusion | bytes 22020096 | tf_op jit(solution)/shard_map/slice | solution.py:122
  276.8 6.2 %fusion.7 = f32[768,512]{1,0:T(8,128)S(1)} fusion(bf16[768,3584]{1,0:T(8,128)(2,1)} %bitcast.159, bf16[2,7168,512]{2,1,0:T(8,128)(2,1)} %bitcast.168), kind=kOutput, calls=%fused_computation.10 | convolution fusion | flops 2818572288 | bytes 10747904 | tf_op jit(solution)/shard_map/dot_general | solution.py:123
  283.1 5.8 %fusion.11 = f32[768,512]{1,0:T(8,128)S(1)} fusion(bf16[768,3584]{1,0:T(8,128)(2,1)S(1)} %bitcast.160, bf16[2,7168,512]{2,1,0:T(8,128)(2,1)} %bitcast.169), kind=kOutput, calls=%fused_computation.14 | convolution fusion | flops 2818572288 | bytes 10747904 | tf_op jit(solution)/shard_map/dot_general | solution.py:123
  289.0 0.2 slice-done.5
  289.2 3.0 add_multiply_fusion.1
  292.2 3.5 select_reduce_fusion.2
  295.7 2.8 fusion.21
  298.5 0.2 stack_reshape.11
  298.7 1.1 stack_reshape.12
  299.7 2.1 copy_bitcast_fusion
  301.9 1.9 reshape.255
  303.7 4.7 all-to-all-start.1
  308.5 182.5 %all-gather.3 = f32[64,4,768]{2,1,0:T(4,128)S(1)} all-gather(f32[1,4,768]{2,1,0:T(4,128)S(1)} %maximum_bitcast_fusion), channel_id=3, replica_groups=mesh['x'=4,'core'=2,'z'=4,'y'=4] {'x','z','y'}, dimensions={0}, use_global_device_ids=true | all-gather | bytes 798720 | tf_op jit(solution)/shard_map/all_gather | solution.py:144
  491.0 1.6 copy.117
  492.7 0.7 constant_dynamic-slice_fusion
  493.6 0.2 fusion.52
  493.9 0.7 copy.119
  494.6 0.5 broadcast_multiply_fusion
  495.2 0.5 copy.116
  495.7 0.4 select_bitcast_fusion
  496.1 2.1 copy.118
  498.1 5.3 %reshape.258 = f32[4,3,65536]{2,0,1:T(4,128)} reshape(f32[4,3,4,2,16,512]{5,4,3,2,0,1:T(8,128)} %copy.118) | data formatting | bytes 6291456 | tf_op jit(solution)/shard_map/reshape | solution.py:169
  (82 shorter events, 2.7 us)
Async XLA Ops:
  7.2 1.3 copy-start
  7.2 1.0 copy-start.3
  7.2 80.9 %all-gather.9.cloned.1.call-start = ((), (), s32[]{:S(2)}) async-start(), calls=%async_computation.3 | async-start | bytes 22020096 | tf_op jit(solution)/shard_map/all_gather | solution.py:77
  8.5 4.5 copy-start.7
  27.8 1.2 copy-start.8
  38.5 8.3 %copy-start.4 = (f32[7168]{0:T(1024)S(1)}, f32[7168]{0:T(1024)}, u32[]{:S(2)}) copy-start(f32[7168]{0:T(1024)} %param.18) | copy-start | bytes 86020
  38.5 49.6 %all-to-all-start = ((bf16[16,24,3584]{2,1,0:T(8,128)(2,1)}), bf16[16,24,3584]{2,1,0:T(8,128)(2,1)}, u32[]{:S(2)}, u32[]{:S(2)}) async-start(bf16[16,24,3584]{2,1,0:T(8,128)(2,1)} %bitcast.154), calls=%async_computation | async-start | bytes 5505024 | tf_op jit(solution)/shard_map/all_to_all | solution.py:98
  46.8 221.1 %all-gather.7.cloned.1.call-start = ((), (), s32[]{:S(2)}) async-start(), calls=%async_computation.2 | async-start | bytes 11182080 | tf_op jit(solution)/shard_map/all_gather | solution.py:112
  88.1 3.9 copy-start.6
  88.1 4.0 copy-start.5
  92.4 1.2 collective-permute-start
  276.8 6.2 %copy-start.2 = (bf16[4,1,192,3584]{3,2,1,0:T(8,128)(2,1)S(1)}, bf16[4,1,192,3584]{3,2,1,0:T(8,128)(2,1)}, u32[]{:S(2)}) copy-start(bf16[4,1,192,3584]{3,2,1,0:T(8,128)(2,1)} %get-tuple-element.39) | copy-start | bytes 16515076
  276.8 12.1 %slice-start = ((s8[5505024]{0:T(1024)(128)(4,1)}), s8[4194304]{0:T(1024)(128)(4,1)S(1)}, s32[]{:S(2)}) async-start(s8[5505024]{0:T(1024)(128)(4,1)} %bitcast.155), calls=%async_computation.4 | async-start | bytes 8388608
  276.8 12.1 %slice-start.2 = ((s8[14680064]{0:T(1024)(128)(4,1)}), s8[4194304]{0:T(1024)(128)(4,1)S(1)}, s32[]{:S(2)}) async-start(s8[14680064]{0:T(1024)(128)(4,1)} %bitcast.170), calls=%async_computation.6 | async-start | bytes 8388608
  276.8 12.1 %slice-start.3 = ((s8[14680064]{0:T(1024)(128)(4,1)}), s8[4194304]{0:T(1024)(128)(4,1)S(1)}, s32[]{:S(2)}) async-start(s8[14680064]{0:T(1024)(128)(4,1)} %bitcast.170), calls=%async_computation.7 | async-start | bytes 8388608
  283.0 5.9 %slice-start.1 = ((s8[5505024]{0:T(1024)(128)(4,1)}), s8[1310720]{0:T(1024)(128)(4,1)S(1)}, s32[]{:S(2)}) async-start(s8[5505024]{0:T(1024)(128)(4,1)} %bitcast.155), calls=%async_computation.5 | async-start | bytes 2621440
  283.1 5.9 %slice-start.4 = ((s8[14680064]{0:T(1024)(128)(4,1)}), s8[4194304]{0:T(1024)(128)(4,1)S(1)}, s32[]{:S(2)}) async-start(s8[14680064]{0:T(1024)(128)(4,1)} %bitcast.170), calls=%async_computation.8 | async-start | bytes 8388608
  283.1 6.1 %slice-start.5 = ((s8[14680064]{0:T(1024)(128)(4,1)}), s8[2097152]{0:T(1024)(128)(4,1)S(1)}, s32[]{:S(2)}) async-start(s8[14680064]{0:T(1024)(128)(4,1)} %bitcast.170), calls=%async_computation.9 | async-start | bytes 4194304
  303.7 191.4 %all-to-all-start.1 = ((bf16[64,24,512]{2,1,0:T(8,128)(2,1)}), bf16[64,24,512]{2,1,0:T(8,128)(2,1)S(1)}, u32[]{:S(2)}, u32[]{:S(2)}) async-start(bf16[64,24,512]{2,1,0:T(8,128)(2,1)} %reshape.255), calls=%async_computation.1 | async-start | bytes 3145728 | tf_op jit(solution)/shard_map/all_to_all | solution.py:150
  498.1 5.3 %copy-start.1 = (bf16[64,3,4,576]{3,2,1,0:T(4,128)(2,1)S(1)}, bf16[64,3,4,576]{3,2,1,0:T(4,128)(2,1)}, u32[]{:S(2)}) copy-start(bf16[64,3,4,576]{3,2,1,0:T(4,128)(2,1)} %param.11) | copy-start | bytes 2654212
Sparse Core Ops, SparseCore 0:
  9.7 32.1 all-gather.8
  92.1 84.2 all-gather.6

commit v3 on v0

v3 whole, which is shorter than its diff:
```python
import functools

import jax
import jax.numpy as jnp
from jax import lax
from jax.experimental import pallas as pl
from jax.experimental.pallas import tpu as pltpu
from jax.sharding import PartitionSpec as P

LAT = 512
DP = ("xh", "xl", "core")
TP = ("z", "y")


score_scale = 192.0 ** (-0.5)
neg_large = -1e30


def attend(lengths, queries_ref, cache_ref, new_ref, up_ref, start, count):
    context = cache_ref.shape[2]
    steps, heads = queries_ref.shape[1:3]
    value = up_ref.shape[2]
    tall = count * 16
    position = lax.broadcasted_iota(jnp.int32, (1, context), 1)
    blank = jnp.zeros((heads, queries_ref.shape[3]), jnp.float32)
    lines = []
    for row in range(start, start + count):
        parts = [queries_ref[row, step].astype(jnp.float32) for step in range(steps)]
        lines.append(jnp.concatenate(parts + [blank], axis=0).astype(jnp.bfloat16))
    latents = jnp.concatenate(
        [new_ref[place].astype(jnp.float32)[start : start + count] for place in range(steps)], axis=0
    ).astype(jnp.bfloat16)
    scores = []
    for row in range(count):
        one = jnp.dot(lines[row], cache_ref[start + row], preferred_element_type=jnp.float32)
        scores.append(jnp.where(position < lengths[row], one * score_scale, neg_large))
    scores = jnp.concatenate(scores, axis=0)
    fresh = lax.dot_general(
        jnp.concatenate(lines, axis=0),
        latents,
        (((1,), (1,)), ((), ())),
        preferred_element_type=jnp.float32,
    )
    line = lax.broadcasted_iota(jnp.int32, fresh.shape, 0)
    key = lax.broadcasted_iota(jnp.int32, fresh.shape, 1)
    step = (line % 16) // 4
    own = jnp.logical_and(line // 16 == key % count, key // count <= step)
    fresh = jnp.where(own, fresh * score_scale, neg_large)
    top = jnp.maximum(
        jnp.max(scores, axis=1, keepdims=True), jnp.max(fresh, axis=1, keepdims=True)
    )
    scores = jnp.exp(scores - top)
    fresh = jnp.exp(fresh - top)
    denom = jnp.sum(scores, axis=1, keepdims=True) + jnp.sum(fresh, axis=1, keepdims=True)
    scores = (scores / denom).astype(jnp.bfloat16)
    fresh = (fresh / denom).astype(jnp.bfloat16)
    latent = []
    for row in range(count):
        latent.append(
            lax.dot_general(
                scores[row * 16 : row * 16 + 16],
                cache_ref[start + row, :LAT, :],
                (((1,), (1,)), ((), ())),
                preferred_element_type=jnp.float32,
            )
        )
    latent = jnp.concatenate(latent, axis=0) + jnp.dot(
        fresh, latents[:, :LAT], preferred_element_type=jnp.float32
    )
    latent = latent.astype(jnp.bfloat16)
    values = jnp.concatenate(
        [jnp.dot(latent, up_ref[head], preferred_element_type=jnp.float32) for head in range(heads)],
        axis=1,
    )
    line = lax.broadcasted_iota(jnp.int32, values.shape, 0)
    entry = lax.broadcasted_iota(jnp.int32, values.shape, 1)
    values = jnp.where(line % 4 == entry // value, values, 0.0).astype(jnp.bfloat16)
    shape = (steps * count, tall)
    target = lax.broadcasted_iota(jnp.int32, shape, 0)
    line = lax.broadcasted_iota(jnp.int32, shape, 1)
    pick = jnp.logical_and(target % count == line // 16, target // count == (line % 16) // 4)
    pick = jnp.where(pick, 1.0, 0.0).astype(jnp.bfloat16)
    return jnp.dot(pick, values, preferred_element_type=jnp.float32)


def attention_kernel(
    lengths_ref, queries_ref, cache_ref, new_ref, up_ref, project_ref, out_ref, values_ref, weight_ref, sems
):
    g = pl.program_id(0)
    parts = sems.shape[0]
    depth = weight_ref.shape[0] // parts
    copies = [
        pltpu.make_async_copy(
            project_ref.at[pl.ds(part * depth, depth)],
            weight_ref.at[pl.ds(part * depth, depth)],
            sems.at[part],
        )
        for part in range(parts)
    ]

    @pl.when(g == 0)
    def _():
        for copy in copies:
            copy.start()

    count = 8
    block = cache_ref.shape[0]
    lengths = [lengths_ref[g * block + row] for row in range(block)]
    values = [
        attend(lengths[start : start + count], queries_ref, cache_ref, new_ref, up_ref, start, count)
        for start in range(0, block, count)
    ]
    values = jnp.concatenate(values, axis=0).astype(jnp.bfloat16)
    lines = values.shape[0]
    values_ref[pl.ds(pl.multiple_of(g * lines, lines), lines), :] = values

    @pl.when(g == pl.num_programs(0) - 1)
    def _():
        for copy in copies:
            copy.wait()
        half = out_ref.shape[2]
        cut = half // 4
        for part in range(8):
            columns = slice((part % 4) * cut, (part % 4 + 1) * cut)
            out_ref[part // 4, :, columns] = jnp.dot(
                values_ref[...],
                weight_ref[:, part * cut : (part + 1) * cut],
                preferred_element_type=jnp.float32,
            ).astype(jnp.bfloat16)


def attention(queries, latent_cache, new_latent, lengths, value_up_weight, out_proj):
    rows, steps, heads, entries = queries.shape
    context = latent_cache.shape[1]
    block = 16
    depth, width = out_proj.shape
    return pl.pallas_call(
        attention_kernel,
        grid_spec=pltpu.PrefetchScalarGridSpec(
            num_scalar_prefetch=1,
            grid=(rows // block,),
            in_specs=[
                pl.BlockSpec((block, steps, heads, entries), lambda g, _: (g, 0, 0, 0)),
                pl.BlockSpec((block, entries, context), lambda g, _: (g, 0, 0)),
                pl.BlockSpec((steps, block, entries), lambda g, _: (0, g, 0)),
                pl.BlockSpec(value_up_weight.shape, lambda g, _: (0, 0, 0)),
                pl.BlockSpec(memory_space=pl.ANY),
            ],
            out_specs=pl.BlockSpec((2, rows * steps, width // 2), lambda g, _: (0, 0, 0)),
            scratch_shapes=[
                pltpu.VMEM((rows * steps, depth), jnp.bfloat16),
                pltpu.VMEM((depth, width), jnp.bfloat16),
                pltpu.SemaphoreType.DMA((4,)),
            ],
        ),
        out_shape=jax.ShapeDtypeStruct((2, rows * steps, width // 2), jnp.bfloat16),
        compiler_params=pltpu.CompilerParams(vmem_limit_bytes=56 * 1024 * 1024),
        cost_estimate=pl.CostEstimate(
            flops=4 * rows * 16 * context * entries + 2 * rows * steps * depth * width,
            bytes_accessed=2 * rows * context * entries + 2 * depth * width,
            transcendentals=rows * 16 * context,
        ),
        name="latent_attention",
    )(
        lengths,
        queries,
        latent_cache.transpose(0, 2, 1),
        new_latent.transpose(1, 0, 2),
        value_up_weight,
        out_proj,
    )


def head_kernel(steps, per_block, k_blocks, width, a_ref, *refs):
    weight_refs = refs[:4]
    meta_ref, gain_ref, out_ref, acc_ref, squares_ref = refs[4:]
    k = pl.program_id(0)

    @pl.when(k == 0)
    def _():
        acc_ref[...] = jnp.zeros_like(acc_ref)
        squares_ref[...] = jnp.zeros_like(squares_ref)

    rows, depth = a_ref.shape[1:]
    vocab = weight_refs[0].shape[1]
    a = a_ref[0]
    for shard, weight_ref in enumerate(weight_refs):
        acc_ref[shard] += jnp.dot(a, weight_ref[...], preferred_element_type=jnp.float32)
    inverse = 1.0 / gain_ref[...]
    wide = a.astype(jnp.float32) * inverse
    wide = wide * wide
    part = wide[:, :128]
    for lane in range(128, depth, 128):
        part = part + wide[:, lane : lane + 128]
    squares_ref[...] += part

    @pl.when(k == k_blocks - 1)
    def _():
        column = lax.broadcasted_iota(jnp.int32, (1, vocab), 1)
        bit = column // (vocab // 16)
        lane = lax.broadcasted_iota(jnp.int32, (1, 128), 1)
        upper = lax.broadcasted_iota(jnp.int32, (1, 8, 1), 1) < 4

        def of_step(full, step):
            return full.reshape(-1, steps, 8, full.shape[1])[:, step]

        def by_owner(first, second):
            count = first.shape[2]
            low = jnp.where(upper, first, pltpu.roll(second, 4, 1))
            high = jnp.where(upper, pltpu.roll(first, 4, 1), second)
            low, high = (one.reshape(-1, 2, 8, count) for one in (low, high))
            return jnp.stack([low, high], axis=1).reshape(-1, count).astype(jnp.bfloat16)

        for block in range(rows // per_block):
            own = pl.ds(block * per_block, per_block)
            to = pl.ds(block * (per_block // steps * 2), per_block // steps * 2)
            square = jnp.sum(squares_ref[own, :], axis=1, keepdims=True)
            norm = lax.rsqrt(square * (1.0 / width) + 1e-06)
            logits, allowed, target, peak = [], [], 0.0, neg_large
            for shard in range(4):
                one = acc_ref[shard, own, :] * norm
                word = meta_ref[shard, own, :]
                is_target = column == meta_ref[4 + shard, own, :]
                open_bit = jnp.bitwise_and(jnp.right_shift(word, bit), 1) == 1
                ok = jnp.logical_or(open_bit, is_target)
                logits.append(one)
                allowed.append(ok)
                target = target + jnp.where(is_target, one, 0.0)
                peak = jnp.maximum(peak, jnp.where(ok, one, neg_large))
            target = jnp.sum(target, axis=1, keepdims=True)
            peak = jnp.max(peak, axis=1, keepdims=True)
            total, moment, sent = 0.0, 0.0, []
            for ok, one in zip(allowed, logits):
                shifted = jnp.where(ok, one - peak, 0.0)
                weight = jnp.where(ok, jnp.exp(shifted), 0.0)
                total = total + weight
                moment = moment + weight * shifted
                sent.append(jnp.where(ok, shifted, 1.0))
            total = jnp.sum(total, axis=1, keepdims=True)
            moment = jnp.sum(moment, axis=1, keepdims=True)
            packed = jnp.zeros((per_block, 128), jnp.float32)
            lanes = 0
            for stat, count in ((peak, 3), (total, 2), (moment, 2), (target, 3)):
                for _ in range(count):
                    piece = stat.astype(jnp.bfloat16).astype(jnp.float32)
                    packed = jnp.where(lane == lanes, piece, packed)
                    stat = stat - piece
                    lanes += 1
            sums = 0.0
            for step in range(steps):
                for two in range(2):
                    start = (step * 2 + two) * vocab
                    out_ref[to, start : start + vocab] = by_owner(
                        of_step(sent[2 * two], step), of_step(sent[2 * two + 1], step)
                    )
                mine = of_step(packed, step)
                sums = sums + (pltpu.roll(mine, step * lanes, 2) if step else mine)
            out_ref[to, steps * 2 * vocab :] = by_owner(sums, sums)


def head(hidden, weights, meta, norm_gain, steps):
    halves, rows, half = hidden.shape
    vocab = weights[0].shape[1]
    depth = half // 2
    k_blocks = halves * 2
    width = halves * half
    out_shape = (rows // steps * 2, steps * 2 * vocab + 128)
    return pl.pallas_call(
        functools.partial(head_kernel, steps, rows // 4, k_blocks, width),
        grid=(k_blocks,),
        in_specs=[pl.BlockSpec((1, rows, depth), lambda k: (k // 2, 0, k % 2))]
        + [pl.BlockSpec((depth, vocab), lambda k: (k, 0))] * 4
        + [
            pl.BlockSpec(meta.shape, lambda k: (0, 0, 0)),
            pl.BlockSpec((1, depth), lambda k: (0, k)),
        ],
        out_specs=pl.BlockSpec(out_shape, lambda k: (0, 0)),
        out_shape=jax.ShapeDtypeStruct(out_shape, jnp.bfloat16),
        scratch_shapes=[
            pltpu.VMEM((4, rows, vocab), jnp.float32),
            pltpu.VMEM((rows, 128), jnp.float32),
        ],
        compiler_params=pltpu.CompilerParams(vmem_limit_bytes=56 * 1024 * 1024),
        cost_estimate=pl.CostEstimate(
            flops=8 * rows * width * vocab,
            bytes_accessed=2 * (rows * width + 4 * width * vocab),
            transcendentals=4 * rows * vocab,
        ),
        name="logits_and_shard_softmax",
    )(hidden, *weights, meta, norm_gain.reshape(1, -1))


def residual_kernel(parts_ref, residual_ref, gain_ref, out_ref):
    summed = residual_ref[...].astype(jnp.float32)
    for part in range(parts_ref.shape[0]):
        summed = summed + parts_ref[part].astype(jnp.float32)
    out_ref[...] = (summed * gain_ref[...]).astype(jnp.bfloat16)


def add_residual(parts, residual, gain):
    return pl.pallas_call(
        residual_kernel,
        out_shape=jax.ShapeDtypeStruct(residual.shape, jnp.bfloat16),
        compiler_params=pltpu.CompilerParams(vmem_limit_bytes=16 * 1024 * 1024),
        cost_estimate=pl.CostEstimate(
            flops=parts.size, bytes_accessed=2 * parts.size, transcendentals=0
        ),
        name="sum_residual_gain",
    )(parts, residual, gain.reshape(1, -1))


def owner_kernel(tp_count, vocab, place_ref, got_ref, out_ref, stats_ref, offset_ref):
    x = pl.program_id(0)
    cores, rows = got_ref.shape[:2]
    steps = out_ref.shape[0]

    @pl.when(x == 0)
    def _():
        packed = got_ref[:, :, steps * 2 * vocab :].astype(jnp.float32)
        lane = lax.broadcasted_iota(jnp.int32, (1, 1, 128), 2)

        def pieces(start, count):
            mine = jnp.logical_and(lane >= start, lane < start + count)
            return jnp.sum(jnp.where(mine, packed, 0.0), axis=2, keepdims=True)

        for step in range(steps):
            first = step * 10
            peaks, totals = pieces(first, 3), pieces(first + 3, 2)
            moments, targets = pieces(first + 5, 2), pieces(first + 7, 3)
            peak = jnp.max(peaks, axis=0, keepdims=True)
            lift = peaks - peak
            scale = jnp.exp(lift)
            total = jnp.sum(scale * totals, axis=0, keepdims=True)
            moment = jnp.sum(scale * (moments + lift * totals), axis=0, keepdims=True)
            target = jnp.sum(targets, axis=0, keepdims=True)
            log_sum = peak + jnp.log(total)
            entropy = jnp.log(total) - moment / total
            stats = jnp.where(lane == 0, entropy, jnp.where(lane == 1, log_sum - target, 0.0))
            stats_ref[step] = stats[0]
            offset_ref[step] = jnp.broadcast_to(peaks - log_sum, (cores, rows, 128))

    x_low, own_core = place_ref[0], place_ref[1]
    two = lax.rem(x + x_low, 2)
    for shard in range(2):
        core = lax.rem(own_core + shard, 2)
        at_x = lax.rem(x + 4 + two * (2 * core - 1), 4)
        for tp in range(tp_count):
            source = tp * 2 + at_x // 2
            start = pl.multiple_of((core * tp_count + tp) * vocab, vocab)
            for step in range(steps):
                from_column = pl.multiple_of((step * 2 + two) * vocab, vocab)
                values = got_ref[source, :, pl.ds(from_column, vocab)].astype(jnp.float32)
                values = jnp.where(values > 0.0, 0.0, values + offset_ref[step, source][:, :1])
                out_ref[step, :, pl.ds(start, vocab)] = values[shard * 4 : shard * 4 + 4]


def owner(place, got, tp_count, vocab, steps):
    rows = got.shape[1]
    cut = 2 * tp_count * vocab
    return pl.pallas_call(
        functools.partial(owner_kernel, tp_count, vocab),
        grid=(4,),
        in_specs=[
            pl.BlockSpec(memory_space=pltpu.SMEM),
            pl.BlockSpec(got.shape, lambda x: (0, 0, 0)),
        ],
        out_specs=[
            pl.BlockSpec((steps, 4, cut), lambda x: (0, 0, x)),
            pl.BlockSpec((steps, rows, 128), lambda x: (0, 0, 0)),
        ],
        out_shape=[
            jax.ShapeDtypeStruct((steps, 4, 4 * cut), jnp.float32),
            jax.ShapeDtypeStruct((steps, rows, 128), jnp.float32),
        ],
        scratch_shapes=[pltpu.VMEM((steps, 2 * tp_count, rows, 128), jnp.float32)],
        compiler_params=pltpu.CompilerParams(vmem_limit_bytes=32 * 1024 * 1024),
        cost_estimate=pl.CostEstimate(
            flops=8 * steps * rows * cut, bytes_accessed=12 * steps * rows * cut, transcendentals=0
        ),
        name="owned_log_probs",
    )(place, got)


def body(
    queries,
    latent_cache,
    new_latent,
    lengths,
    value_up_weight,
    out_proj,
    residual,
    norm_gain,
    head_weight,
    mask_bits,
    targets,
):
    rows, steps = queries.shape[:2]
    width = residual.shape[2]
    half = width // 2
    vocab_dev = head_weight.shape[1]
    tp_count, groups = lax.axis_size(TP), lax.axis_size(TP) // 2
    group_rows = rows // groups
    pairs = steps * group_rows
    x_high, x_low, core = (lax.axis_index(axis) for axis in DP)
    x, tp = 2 * x_high + x_low, lax.axis_index(TP)

    def other_core(value):
        return lax.ppermute(value, "core", ((0, 1), (1, 0)))

    def next_chip(value):
        return lax.ppermute(
            value, DP, tuple(((i + 2 - 4 * (i % 2)) % 8, i) for i in range(8))
        )

    def four(own):
        near = next_chip(own)
        return [own, other_core(own), near, other_core(near)]

    weights = four(head_weight)
    shard_x = jnp.stack([x, x, x + 1 - 2 * core, x - 1 + 2 * core]) % 4
    shard = (2 * shard_x + jnp.stack([core, 1 - core, core, 1 - core])) * tp_count + tp

    def rows_here(full):
        cut = full.reshape(2, 2, 2, groups, group_rows, steps)
        cut = lax.dynamic_slice(
            cut, (0, x_low, core, 0, 0, 0), (2, 1, 1, groups, group_rows, steps)
        )
        return cut.reshape(2, groups, group_rows, steps).transpose(1, 0, 3, 2).reshape(-1)

    words = [rows_here(one) for one in four(mask_bits.reshape(-1, steps))]
    local_targets = rows_here(targets) - (shard * vocab_dev)[:, None]
    meta = jnp.concatenate([jnp.stack(words), local_targets])[..., None]

    partial = attention(
        queries, latent_cache, new_latent, lengths, value_up_weight, out_proj
    )
    own_half, own_group = tp // groups, tp % groups
    resid = lax.dynamic_slice(
        residual.transpose(1, 0, 2),
        (0, own_group * group_rows, own_half * half),
        (steps, group_rows, half),
    ).reshape(pairs, half)
    gain = lax.dynamic_slice_in_dim(norm_gain, own_half * half, half, 0)
    attn = lax.all_to_all(
        partial.reshape(tp_count, pairs, half), TP, split_axis=0, concat_axis=0, tiled=True
    )
    hidden = add_residual(attn, resid, gain)
    across = lax.ppermute(hidden, "xh", ((0, 1), (1, 0)))
    hidden = jnp.where(x_high == 0, jnp.stack([hidden, across]), jnp.stack([across, hidden]))
    hidden = lax.all_gather(hidden, TP, axis=0).reshape(2, groups * 2 * pairs, half)
    sent = head(hidden, weights, meta, norm_gain, steps)
    sent = sent.reshape(tp_count * 2, 8, -1)
    sent = lax.all_to_all(sent, ("z", "y", "xh"), split_axis=0, concat_axis=0, tiled=True)
    log_probs, stats = owner(jnp.stack([x_low, core]), sent, tp_count, vocab_dev, steps)
    own_rows = rows // tp_count
    entropy = stats[:, :own_rows, 0].T
    row_loss = jnp.mean(stats[:, :own_rows, 1], axis=0)
    return (log_probs.transpose(1, 0, 2), entropy, row_loss)


def solution(mesh):
    axes = DP + TP
    mesh = jax.sharding.Mesh(mesh.devices.reshape(2, 2, 2, 4, 4), axes)
    placed = (
        P(DP, None, TP, None),
        P(DP, None, None),
        P(DP, None, None),
        P(DP),
        P(TP, None, None),
        P(TP, None),
        P(DP, None, None),
        P(),
        P(None, axes),
        P(None, None, axes),
        P(),
    )
    return jax.shard_map(
        body,
        mesh=mesh,
        in_specs=placed,
        out_specs=(P(axes, None, None), P(axes, None), P(axes)),
        check_vma=False,
    )
```

time: 468 us -> 224 us (0.48)
  blocking collectives: 129 us -> 0 us
  waiting for transfers between devices: 244 us -> 121 us
  matrix products: 48 us -> 0 us
  Pallas kernels: 0 us -> 47.2 us
  starting transfers between devices: 5.1 us -> 36.4 us
  other arithmetic: 12.7 us -> 1.74 us
  local copies, waits for them, and re-layouts: 12.6 us -> 3.62 us
    unnamed x3 -> x1, waiting for transfers between devices: 116 us -> 0.02 us
    pmax x1 -> x0, blocking collectives: 64.8 us -> none  [body(): peak = lax.pmax(jnp.max(masked, axis=-1), ('dp', 'tp'))]
    psum x1 -> x0, blocking collectives: 64.6 us -> none  [body(): lax.psum((jnp.sum(weights, axis=-1), jnp.sum(weights * shifted, axis=-1),...]
    all_gather x1, waiting for transfers between devices: 99.7 us -> 45 us  [body(): lax.all_gather(hidden, TP, axis=0).reshape(2, groups * 2 * pairs, half)]
    dot_general x7 -> x0, matrix products: 48 us -> none  [the longest x1 22.5 us: body(): jnp.dot(lax.all_gather(hidden, ('dp', 'tp'), axis=0, tiled=True), head_we...]
    pallas_call x0 -> x4, Pallas kernels: none -> 47.2 us  [the longest x1 23.1 us: head(): pl.pallas_call(functools.partial(head_kernel, steps, rows // 4, k_blocks,...]
    all_to_all x1 -> x2, waiting for transfers between devices: 28.4 us -> 62.5 us  [the longest x1 36.9 us: body(): lax.all_to_all(partial.reshape(tp_count, pairs, half), TP, split_axis=0,...]
    ppermute x0 -> x7, starting transfers between devices: none -> 20.2 us  [the longest x4 8.78 us: other_core(): return lax.ppermute(value, 'core', ((0, 1), (1, 0)))]
  transfers between devices with their start and end apart: 3 -> 10, of which waited for: 3 -> 6; matrix products, arithmetic and copies ran while one was open for 0% -> 2% of each run, Pallas kernels for 0% -> 9%
where the time goes in v3:
time: 224 us
  waiting for transfers between devices  121 us (54%)
  Pallas kernels  47.2 us (21%)
  starting transfers between devices  36.4 us (16%)
  between operations  14.3 us (6%)
  local copies, waits for them, and re-layouts  3.62 us (2%)
    all_gather x1, waiting for transfers between devices, body(): lax.all_gather(hidden, TP, axis=0).reshape(2, groups * 2 * pairs, half)  45 us
    all_to_all x1, waiting for transfers between devices, body(): lax.all_to_all(partial.reshape(tp_count, pairs, half), TP, split_axis=0,...  36.9 us
    all_to_all x1, waiting for transfers between devices, body(): lax.all_to_all(sent, ('z', 'y', 'xh'), split_axis=0, concat_axis=0, tiled...  25.6 us
    pallas_call x1, Pallas kernels, head(): pl.pallas_call(functools.partial(head_kernel, steps, rows // 4, k_blocks,...  23.1 us
    pallas_call x1, Pallas kernels, attention(): pl.pallas_call(attention_kernel, grid_spec=pltpu.PrefetchScalarGridSpec(n...  17.1 us
    ppermute x4, starting transfers between devices, other_core(): return lax.ppermute(value, 'core', ((0, 1), (1, 0)))  8.78 us
    all_to_all x1, starting transfers between devices, body(): lax.all_to_all(partial.reshape(tp_count, pairs, half), TP, split_axis=0,...  8.11 us
    all_to_all x1, starting transfers between devices, body(): lax.all_to_all(sent, ('z', 'y', 'xh'), split_axis=0, concat_axis=0, tiled...  8.1 us
  transfers between devices with their start and end apart: 10, of which 6 were waited for; matrix products, arithmetic and copies ran while one was open for 2% of the time, Pallas kernels for 9%

profile of v3, /device:TPU:0, one launch (start us, length us, event | category | flops | bytes accessed | tf_op | source)
XLA Modules:
  0.0 224.1 jit_solution(6240112535653241166)
XLA Ops:
  7.2 0.0 copy-start
  7.2 2.9 %collective-permute-start.2 = (bf16[7168,512]{1,0:T(8,128)(2,1)}, bf16[7168,512]{1,0:T(8,128)(2,1)}, u32[]{:S(2)}, u32[]{:S(2)}) collective-permute-start(bf16[7168,512]{1,0:T(8,128)(2,1)} %refs_0_.1), channel_id=1, source_target_pairs={{32,0},{112,16},{64,32},{16,48},{96,64},{48,80},{0,96},{80,112},{3... | collective-permute-start | bytes 22020104 | tf_op jit(solution)/shard_map/ppermute | solution.py:411
  10.1 17.1 %latent_attention.1 = bf16[2,192,3584]{2,1,0:T(8,128)(2,1)} custom-call(s32[64]{0:T(128)} %lengths_ref.1, bf16[64,3,4,576]{3,2,1,0:T(4,128)(2,1)} %queries_ref.1, bf16[64,576,128]{2,1,0:T(8,128)(2,1)} %bitcast.61, bf16[3,64,576]{2,1,0:T(8,128)(2,1)} %bitcast.63, bf16[4,512,128]{2,1,0:T(8,128)(2,1)} %up_ref.1, bf16[512,7168]{1,0:T(8,128)(2,1)} %project_ref.1), custom_call_target="tpu_custom_call" | custom-call | flops 1711276032 | bytes 16777216 | tf_op jit(solution)/shard_map/latent_attention/pallas_call | solution.py:137
  27.2 0.0 copy-start.3
  27.2 8.1 %all-to-all-start = ((bf16[16,24,3584]{2,1,0:T(8,128)(2,1)}), bf16[16,24,3584]{2,1,0:T(8,128)(2,1)}, u32[]{:S(2)}, u32[]{:S(2)}) async-start(bf16[16,24,3584]{2,1,0:T(8,128)(2,1)} %bitcast.60), calls=%async_computation | async-start | bytes 5505024 | tf_op jit(solution)/shard_map/all_to_all | solution.py:444
  35.3 0.0 copy-start.2
  35.3 0.0 copy-start.4
  35.3 0.0 all-gather.2.cloned.1.call-start
  35.4 0.1 dynamic_slice.22
  35.6 36.9 %all-to-all-done.parts_ref = bf16[16,24,3584]{2,1,0:T(8,128)(2,1)} async-done(((bf16[16,24,3584]{2,1,0:T(8,128)(2,1)}), bf16[16,24,3584]{2,1,0:T(8,128)(2,1)}, u32[]{:S(2)}, u32[]{:S(2)}) %all-to-all-start) | async-done | bytes 2752544 | tf_op jit(solution)/shard_map/all_to_all | solution.py:444
  72.5 2.2 sum_residual_gain.1
  74.7 6.2 %collective-permute-start = (bf16[24,3584]{1,0:T(8,128)(2,1)S(1)}, bf16[24,3584]{1,0:T(8,128)(2,1)S(1)}, u32[]{:S(2)}, u32[]{:S(2)}) collective-permute-start(bf16[24,3584]{1,0:T(8,128)(2,1)S(1)} %sum_residual_gain.1), channel_id=1, source_target_pairs={{0,64},{64,0},{1,65},{65,1},{2,66},{66,2},{3,67},{67,3},{4,68},{68... | collective-permute-start | bytes 516104 | tf_op jit(solution)/shard_map/ppermute | solution.py:448
  80.9 5.3 %collective-permute-done = bf16[24,3584]{1,0:T(8,128)(2,1)S(1)} collective-permute-done((bf16[24,3584]{1,0:T(8,128)(2,1)S(1)}, bf16[24,3584]{1,0:T(8,128)(2,1)S(1)}, u32[]{:S(2)}, u32[]{:S(2)}) %collective-permute-start) | collective-permute-done | bytes 172064 | tf_op jit(solution)/shard_map/ppermute | solution.py:448
  86.2 0.8 maximum_select_fusion
  87.0 0.0 all-gather.2.cloned.1.call-update
  87.0 8.2 %collective-permute-start.1 = (bf16[7168,512]{1,0:T(8,128)(2,1)}, bf16[7168,512]{1,0:T(8,128)(2,1)}, u32[]{:S(2)}, u32[]{:S(2)}) collective-permute-start(bf16[7168,512]{1,0:T(8,128)(2,1)} %refs_0_.1), channel_id=1, source_target_pairs={{0,16},{16,0},{1,17},{17,1},{2,18},{18,2},{3,19},{19,3},{4,20},{20... | collective-permute-start | bytes 22020104 | tf_op jit(solution)/shard_map/ppermute | solution.py:408
  95.2 0.0 collective-permute-done.2.refs_2_
  95.2 0.1 collective-permute-start.3
  95.3 2.3 %collective-permute-start.5 = (s32[512,3]{0,1:T(4,128)S(1)}, s32[512,3]{0,1:T(4,128)S(1)}, u32[]{:S(2)}, u32[]{:S(2)}) collective-permute-start(s32[512,3]{0,1:T(4,128)S(1)} %bitcast.72), channel_id=1, source_target_pairs={{32,0},{112,16},{64,32},{16,48},{96,64},{48,80},{0,96},{80,112},{3... | collective-permute-start | bytes 18440 | tf_op jit(solution)/shard_map/ppermute | solution.py:411
  97.6 0.0 collective-permute-start.4
  97.6 0.1 add_multiply_fusion
  97.7 0.1 reshape_reshape.3
  97.8 0.1 reshape.254
  98.0 1.0 collective-permute-done.5
  99.0 0.5 collective-permute-start.6
  99.4 0.1 reshape.250
  99.5 7.0 %collective-permute-done.4 = s32[512,3]{0,1:T(4,128)S(1)} collective-permute-done((s32[512,3]{0,1:T(4,128)S(1)}, s32[512,3]{0,1:T(4,128)S(1)}, u32[]{:S(2)}, u32[]{:S(2)}) %collective-permute-start.4) | collective-permute-done | bytes 6176 | tf_op jit(solution)/shard_map/ppermute | solution.py:408
  106.5 0.1 reshape.248
  106.7 0.1 stack_reshape.13
  106.8 0.1 stack_reshape.12
  106.9 0.1 stack_reshape.14
  107.0 0.0 collective-permute-done.6
  107.0 0.1 reshape.252
  107.2 0.1 sub.30
  107.3 0.1 stack_reshape.15
  107.4 0.1 broadcast_subtract_fusion
  107.5 1.7 copy.31.refs_4_
  109.2 0.0 collective-permute-done.1.refs_1_
  109.2 45.0 %all-gather.2.cloned.1.call-done = bf16[16,2,24,3584]{3,2,1,0:T(8,128)(2,1)} async-done(((bf16[1,2,24,3584]{3,2,1,0:T(8,128)(2,1)}), bf16[16,2,24,3584]{3,2,1,0:T(8,128)(2,1)}) %all-gather.2.cloned.1.call-update) | async-done | bytes 5505040 | tf_op jit(solution)/shard_map/all_gather | solution.py:450
  154.2 0.0 collective-permute-done.3.refs_3_
  154.2 23.1 %logits_and_shard_softmax.1 = bf16[256,3200]{1,0:T(8,128)(2,1)} custom-call(bf16[2,384,3584]{2,1,0:T(8,128)(2,1)} %bitcast.75, bf16[7168,512]{1,0:T(8,128)(2,1)} %refs_0_.1, bf16[7168,512]{1,0:T(8,128)(2,1)} %collective-permute-done.1.refs_1_, bf16[7168,512]{1,0:T(8,128)(2,1)} %collective-permute-done.2.refs_2_, ...), custom_call_target="tpu_custom_call" | custom-call | flops 11274289152 | bytes 34865152 | tf_op jit(solution)/shard_map/logits_and_shard_softmax/pallas_call | solution.py:268
  177.3 8.1 %all-to-all-start.1 = ((bf16[32,8,3200]{2,1,0:T(8,128)(2,1)}), bf16[32,8,3200]{2,1,0:T(8,128)(2,1)}, u32[]{:S(2)}, u32[]{:S(2)}) async-start(bf16[32,8,3200]{2,1,0:T(8,128)(2,1)} %bitcast.62), calls=%async_computation.1 | async-start | bytes 3276800 | tf_op jit(solution)/shard_map/all_to_all | solution.py:453
  185.4 0.1 pad_add_fusion.place_ref
  185.5 25.6 %all-to-all-done.1.got_ref = bf16[32,8,3200]{2,1,0:T(8,128)(2,1)} async-done(((bf16[32,8,3200]{2,1,0:T(8,128)(2,1)}), bf16[32,8,3200]{2,1,0:T(8,128)(2,1)}, u32[]{:S(2)}, u32[]{:S(2)}) %all-to-all-start.1) | async-done | bytes 1638432 | tf_op jit(solution)/shard_map/all_to_all | solution.py:453
  211.1 4.8 %owned_log_probs.1 = (f32[3,4,65536]{2,1,0:T(4,128)}, f32[3,8,128]{2,1,0:T(8,128)S(1)}) custom-call(s32[2]{0:T(128)S(1)} %pad_add_fusion.place_ref, bf16[32,8,3200]{2,1,0:T(8,128)(2,1)} %all-to-all-done.1.got_ref), custom_call_target="tpu_custom_call" | custom-call | flops 3145728 | bytes 4718592 | tf_op jit(solution)/shard_map/owned_log_probs/pallas_call | solution.py:360
  215.9 0.2 slice_reduce_fusion
  216.1 0.5 broadcast_multiply_fusion
  216.6 0.7 copy.32
  (19 shorter events, 0.2 us)
Async XLA Ops:
  7.2 28.4 %copy-start = (bf16[64,3,7168]{2,0,1:T(8,128)(2,1)S(1)}, bf16[64,3,7168]{2,0,1:T(8,128)(2,1)}, u32[]{:S(2)}) copy-start(bf16[64,3,7168]{2,0,1:T(8,128)(2,1)} %param.17) | copy-start | bytes 8257540
  7.2 88.0 %collective-permute-start.2 = (bf16[7168,512]{1,0:T(8,128)(2,1)}, bf16[7168,512]{1,0:T(8,128)(2,1)}, u32[]{:S(2)}, u32[]{:S(2)}) collective-permute-start(bf16[7168,512]{1,0:T(8,128)(2,1)} %refs_0_.1), channel_id=1, source_target_pairs={{32,0},{112,16},{64,32},{16,48},{96,64},{48,80},{0,96},{80,112},{3... | collective-permute-start | bytes 22020104 | tf_op jit(solution)/shard_map/ppermute | solution.py:411
  27.2 8.2 %copy-start.3 = (f32[7168]{0:T(1024)S(1)}, f32[7168]{0:T(1024)}, u32[]{:S(2)}) copy-start(f32[7168]{0:T(1024)} %param.18) | copy-start | bytes 86020
  27.2 45.3 %all-to-all-start = ((bf16[16,24,3584]{2,1,0:T(8,128)(2,1)}), bf16[16,24,3584]{2,1,0:T(8,128)(2,1)}, u32[]{:S(2)}, u32[]{:S(2)}) async-start(bf16[16,24,3584]{2,1,0:T(8,128)(2,1)} %bitcast.60), calls=%async_computation | async-start | bytes 5505024 | tf_op jit(solution)/shard_map/all_to_all | solution.py:444
  35.3 60.0 %copy-start.2 = (s32[512,3,1]{0,2,1:T(1,128)S(1)}, s32[512,3,1]{0,2,1:T(1,128)}, u32[]{:S(2)}) copy-start(s32[512,3,1]{0,2,1:T(1,128)} %param.20) | copy-start | bytes 18436
  35.3 62.5 %copy-start.4 = (s32[512,3]{0,1:T(4,128)S(1)}, s32[512,3]{0,1:T(4,128)}, u32[]{:S(2)}) copy-start(s32[512,3]{0,1:T(4,128)} %param.21) | copy-start | bytes 18436
  35.3 118.9 %all-gather.2.cloned.1.call-start = ((), (), s32[]{:S(2)}) async-start(), calls=%async_computation.2 | async-start | bytes 5849088 | tf_op jit(solution)/shard_map/all_gather | solution.py:450
  74.7 11.5 %collective-permute-start = (bf16[24,3584]{1,0:T(8,128)(2,1)S(1)}, bf16[24,3584]{1,0:T(8,128)(2,1)S(1)}, u32[]{:S(2)}, u32[]{:S(2)}) collective-permute-start(bf16[24,3584]{1,0:T(8,128)(2,1)S(1)} %sum_residual_gain.1), channel_id=1, source_target_pairs={{0,64},{64,0},{1,65},{65,1},{2,66},{66,2},{3,67},{67,3},{4,68},{68... | collective-permute-start | bytes 516104 | tf_op jit(solution)/shard_map/ppermute | solution.py:448
  87.0 22.2 %collective-permute-start.1 = (bf16[7168,512]{1,0:T(8,128)(2,1)}, bf16[7168,512]{1,0:T(8,128)(2,1)}, u32[]{:S(2)}, u32[]{:S(2)}) collective-permute-start(bf16[7168,512]{1,0:T(8,128)(2,1)} %refs_0_.1), channel_id=1, source_target_pairs={{0,16},{16,0},{1,17},{17,1},{2,18},{18,2},{3,19},{19,3},{4,20},{20... | collective-permute-start | bytes 22020104 | tf_op jit(solution)/shard_map/ppermute | solution.py:408
  95.2 59.0 %collective-permute-start.3 = (bf16[7168,512]{1,0:T(8,128)(2,1)}, bf16[7168,512]{1,0:T(8,128)(2,1)}, u32[]{:S(2)}, u32[]{:S(2)}) collective-permute-start(bf16[7168,512]{1,0:T(8,128)(2,1)} %collective-permute-done.2.refs_2_), channel_id=1, source_target_pairs={{0,16},{16,0},{1,17},{17,1},{2,18},{18,2},{3,19},{19,3},{4,20},{20... | collective-permute-start | bytes 22020104 | tf_op jit(solution)/shard_map/ppermute | solution.py:408
  95.3 3.7 %collective-permute-start.5 = (s32[512,3]{0,1:T(4,128)S(1)}, s32[512,3]{0,1:T(4,128)S(1)}, u32[]{:S(2)}, u32[]{:S(2)}) collective-permute-start(s32[512,3]{0,1:T(4,128)S(1)} %bitcast.72), channel_id=1, source_target_pairs={{32,0},{112,16},{64,32},{16,48},{96,64},{48,80},{0,96},{80,112},{3... | collective-permute-start | bytes 18440 | tf_op jit(solution)/shard_map/ppermute | solution.py:411
  97.6 8.9 %collective-permute-start.4 = (s32[512,3]{0,1:T(4,128)S(1)}, s32[512,3]{0,1:T(4,128)S(1)}, u32[]{:S(2)}, u32[]{:S(2)}) collective-permute-start(s32[512,3]{0,1:T(4,128)S(1)} %bitcast.73), channel_id=1, source_target_pairs={{0,16},{16,0},{1,17},{17,1},{2,18},{18,2},{3,19},{19,3},{4,20},{20... | collective-permute-start | bytes 18440 | tf_op jit(solution)/shard_map/ppermute | solution.py:408
  99.0 8.1 %collective-permute-start.6 = (s32[512,3]{0,1:T(4,128)S(1)}, s32[512,3]{0,1:T(4,128)S(1)}, u32[]{:S(2)}, u32[]{:S(2)}) collective-permute-start(s32[512,3]{0,1:T(4,128)S(1)} %collective-permute-done.5), channel_id=1, source_target_pairs={{0,16},{16,0},{1,17},{17,1},{2,18},{18,2},{3,19},{19,3},{4,20},{20... | collective-permute-start | bytes 18440 | tf_op jit(solution)/shard_map/ppermute | solution.py:408
  154.2 63.0 %copy-start.1 = (bf16[64,3,7168]{2,0,1:T(8,128)(2,1)S(1)}, bf16[64,3,7168]{2,0,1:T(8,128)(2,1)}, u32[]{:S(2)}) copy-start(bf16[64,3,7168]{2,0,1:T(8,128)(2,1)} %param.17) | copy-start | bytes 8257540
  177.3 33.8 %all-to-all-start.1 = ((bf16[32,8,3200]{2,1,0:T(8,128)(2,1)}), bf16[32,8,3200]{2,1,0:T(8,128)(2,1)}, u32[]{:S(2)}, u32[]{:S(2)}) async-start(bf16[32,8,3200]{2,1,0:T(8,128)(2,1)} %bitcast.62), calls=%async_computation.1 | async-start | bytes 3276800 | tf_op jit(solution)/shard_map/all_to_all | solution.py:453
Sparse Core Ops, SparseCore 0:
  87.1 67.0 all-gather.1

commit v4 on v3

--- a/solution.py
+++ b/solution.py
@@ -84,7 +84,19 @@
 
 
 def attention_kernel(
-    lengths_ref, queries_ref, cache_ref, new_ref, up_ref, project_ref, out_ref, values_ref, weight_ref, sems
+    lengths_ref,
+    queries_ref,
+    cache_ref,
+    new_ref,
+    up_ref,
+    project_ref,
+    head_ref,
+    out_ref,
+    first_ref,
+    second_ref,
+    values_ref,
+    weight_ref,
+    sems,
 ):
     g = pl.program_id(0)
     parts = sems.shape[0]
@@ -97,11 +109,20 @@
         )
         for part in range(parts)
     ]
-
     @pl.when(g == 0)
     def _():
         for copy in copies:
             copy.start()
+
+    middle = pl.num_programs(0) // 2
+
+    @pl.when(g < middle)
+    def _():
+        first_ref[...] = head_ref[...]
+
+    @pl.when(g >= middle)
+    def _():
+        second_ref[...] = head_ref[...]
 
     count = 8
     block = cache_ref.shape[0]
@@ -129,31 +150,41 @@
             ).astype(jnp.bfloat16)
 
 
-def attention(queries, latent_cache, new_latent, lengths, value_up_weight, out_proj):
+def attention(queries, latent_cache, new_latent, lengths, value_up_weight, out_proj, head_weight):
     rows, steps, heads, entries = queries.shape
     context = latent_cache.shape[1]
     block = 16
+    grid = rows // block
     depth, width = out_proj.shape
+    head_block = (width // grid, head_weight.shape[1])
     return pl.pallas_call(
         attention_kernel,
         grid_spec=pltpu.PrefetchScalarGridSpec(
             num_scalar_prefetch=1,
-            grid=(rows // block,),
+            grid=(grid,),
             in_specs=[
                 pl.BlockSpec((block, steps, heads, entries), lambda g, _: (g, 0, 0, 0)),
                 pl.BlockSpec((block, entries, context), lambda g, _: (g, 0, 0)),
                 pl.BlockSpec((steps, block, entries), lambda g, _: (0, g, 0)),
                 pl.BlockSpec(value_up_weight.shape, lambda g, _: (0, 0, 0)),
                 pl.BlockSpec(memory_space=pl.ANY),
+                pl.BlockSpec(head_block, lambda g, _: (g, 0)),
             ],
-            out_specs=pl.BlockSpec((2, rows * steps, width // 2), lambda g, _: (0, 0, 0)),
+            out_specs=[
+                pl.BlockSpec((2, rows * steps, width // 2), lambda g, _: (0, 0, 0)),
+                pl.BlockSpec(head_block, lambda g, _: (jnp.minimum(g, grid // 2 - 1), 0)),
+                pl.BlockSpec(head_block, lambda g, _: (jnp.maximum(g - grid // 2, 0), 0)),
+            ],
             scratch_shapes=[
                 pltpu.VMEM((rows * steps, depth), jnp.bfloat16),
                 pltpu.VMEM((depth, width), jnp.bfloat16),
                 pltpu.SemaphoreType.DMA((4,)),
             ],
         ),
-        out_shape=jax.ShapeDtypeStruct((2, rows * steps, width // 2), jnp.bfloat16),
+        out_shape=[
+            jax.ShapeDtypeStruct((2, rows * steps, width // 2), jnp.bfloat16),
+        ]
+        + [jax.ShapeDtypeStruct((width // 2, head_weight.shape[1]), jnp.bfloat16)] * 2,
         compiler_params=pltpu.CompilerParams(vmem_limit_bytes=56 * 1024 * 1024),
         cost_estimate=pl.CostEstimate(
             flops=4 * rows * 16 * context * entries + 2 * rows * steps * depth * width,
@@ -168,12 +199,30 @@
         new_latent.transpose(1, 0, 2),
         value_up_weight,
         out_proj,
-    )
+        head_weight,
+    )
+
+
+def nothing_kernel(value_ref, after_ref, out_ref):
+    pass
+
+
+def once(value, after):
+    anywhere = pl.BlockSpec(memory_space=pl.ANY)
+    return pl.pallas_call(
+        nothing_kernel,
+        in_specs=[anywhere, anywhere],
+        out_specs=anywhere,
+        out_shape=jax.ShapeDtypeStruct(value.shape, value.dtype),
+        input_output_aliases={0: 0},
+        name="value_after",
+    )(value, after)
 
 
 def head_kernel(steps, per_block, k_blocks, width, a_ref, *refs):
-    weight_refs = refs[:4]
-    meta_ref, gain_ref, out_ref, acc_ref, squares_ref = refs[4:]
+    weight_refs = refs[:2]
+    moved_refs = refs[2:6]
+    meta_ref, gain_ref, out_ref, acc_ref, squares_ref = refs[6:]
     k = pl.program_id(0)
 
     @pl.when(k == 0)
@@ -186,6 +235,16 @@
     a = a_ref[0]
     for shard, weight_ref in enumerate(weight_refs):
         acc_ref[shard] += jnp.dot(a, weight_ref[...], preferred_element_type=jnp.float32)
+    for part in range(2):
+
+        @pl.when(k // (k_blocks // 2) == part)
+        def _(part=part):
+            for shard in range(2):
+                weight_ref = moved_refs[2 * shard + part]
+                acc_ref[2 + shard] += jnp.dot(
+                    a, weight_ref[...], preferred_element_type=jnp.float32
+                )
+
     inverse = 1.0 / gain_ref[...]
     wide = a.astype(jnp.float32) * inverse
     wide = wide * wide
@@ -269,7 +328,12 @@
         functools.partial(head_kernel, steps, rows // 4, k_blocks, width),
         grid=(k_blocks,),
         in_specs=[pl.BlockSpec((1, rows, depth), lambda k: (k // 2, 0, k % 2))]
-        + [pl.BlockSpec((depth, vocab), lambda k: (k, 0))] * 4
+        + [pl.BlockSpec((depth, vocab), lambda k: (k, 0))] * 2
+        + [
+            pl.BlockSpec((depth, vocab), lambda k: (jnp.minimum(k, k_blocks // 2 - 1), 0)),
+            pl.BlockSpec((depth, vocab), lambda k: (jnp.maximum(k - k_blocks // 2, 0), 0)),
+        ]
+        * 2
         + [
             pl.BlockSpec(meta.shape, lambda k: (0, 0, 0)),
             pl.BlockSpec((1, depth), lambda k: (0, k)),
@@ -290,23 +354,26 @@
     )(hidden, *weights, meta, norm_gain.reshape(1, -1))
 
 
-def residual_kernel(parts_ref, residual_ref, gain_ref, out_ref):
+def residual_kernel(parts_ref, residual_ref, gain_ref, after_ref, out_ref):
     summed = residual_ref[...].astype(jnp.float32)
     for part in range(parts_ref.shape[0]):
         summed = summed + parts_ref[part].astype(jnp.float32)
     out_ref[...] = (summed * gain_ref[...]).astype(jnp.bfloat16)
 
 
-def add_residual(parts, residual, gain):
+def add_residual(parts, residual, gain, after):
+    in_vmem = pl.BlockSpec(memory_space=pltpu.VMEM)
     return pl.pallas_call(
         residual_kernel,
+        in_specs=[in_vmem, in_vmem, in_vmem, pl.BlockSpec(memory_space=pl.ANY)],
+        out_specs=in_vmem,
         out_shape=jax.ShapeDtypeStruct(residual.shape, jnp.bfloat16),
         compiler_params=pltpu.CompilerParams(vmem_limit_bytes=16 * 1024 * 1024),
         cost_estimate=pl.CostEstimate(
             flops=parts.size, bytes_accessed=2 * parts.size, transcendentals=0
         ),
         name="sum_residual_gain",
-    )(parts, residual, gain.reshape(1, -1))
+    )(parts, residual, gain.reshape(1, -1), after)
 
 
 def owner_kernel(tp_count, vocab, place_ref, got_ref, out_ref, stats_ref, offset_ref):
@@ -416,7 +483,6 @@
         near = next_chip(own)
         return [own, other_core(own), near, other_core(near)]
 
-    weights = four(head_weight)
     shard_x = jnp.stack([x, x, x + 1 - 2 * core, x - 1 + 2 * core]) % 4
     shard = (2 * shard_x + jnp.stack([core, 1 - core, core, 1 - core])) * tp_count + tp
 
@@ -431,8 +497,8 @@
     local_targets = rows_here(targets) - (shard * vocab_dev)[:, None]
     meta = jnp.concatenate([jnp.stack(words), local_targets])[..., None]
 
-    partial = attention(
-        queries, latent_cache, new_latent, lengths, value_up_weight, out_proj
+    partial, first_half, second_half = attention(
+        queries, latent_cache, new_latent, lengths, value_up_weight, out_proj, head_weight
     )
     own_half, own_group = tp // groups, tp % groups
     resid = lax.dynamic_slice(
@@ -444,9 +510,12 @@
     attn = lax.all_to_all(
         partial.reshape(tp_count, pairs, half), TP, split_axis=0, concat_axis=0, tiled=True
     )
-    hidden = add_residual(attn, resid, gain)
+    near = next_chip(first_half)
+    hidden = add_residual(attn, resid, gain, near)
     across = lax.ppermute(hidden, "xh", ((0, 1), (1, 0)))
     hidden = jnp.where(x_high == 0, jnp.stack([hidden, across]), jnp.stack([across, hidden]))
+    near = [near, next_chip(once(second_half, hidden))]
+    weights = [head_weight, other_core(head_weight)] + near + [other_core(one) for one in near]
     hidden = lax.all_gather(hidden, TP, axis=0).reshape(2, groups * 2 * pairs, half)
     sent = head(hidden, weights, meta, norm_gain, steps)
     sent = sent.reshape(tp_count * 2, 8, -1)

time: 224 us -> 218 us (0.973)
  waiting for transfers between devices: 121 us -> 113 us
  Pallas kernels: 47.2 us -> 52.4 us
  starting transfers between devices: 36.4 us -> 32.1 us
    all_gather x1, waiting for transfers between devices: 45 us -> 2.66 us  [body(): lax.all_gather(hidden, TP, axis=0).reshape(2, groups * 2 * pairs, half)]
    ppermute x2 -> x3, waiting for transfers between devices: 1.01 us -> 42 us  [next_chip(): lax.ppermute(value, DP, tuple((((i + 2 - 4 * (i % 2)) % 8, i) for i in ra...]
    ppermute x4 -> x5, starting transfers between devices: 8.78 us -> 1.4 us  [other_core(): return lax.ppermute(value, 'core', ((0, 1), (1, 0)))]
    ppermute x4 -> x5, waiting for transfers between devices: 6.97 us -> 1.69 us  [other_core(): return lax.ppermute(value, 'core', ((0, 1), (1, 0)))]
    pallas_call x1, Pallas kernels: 23.1 us -> 26.3 us  [head(): pl.pallas_call(functools.partial(head_kernel, steps, rows // 4, k_blocks,...]
    ppermute x2 -> x3, starting transfers between devices: 5.2 us -> 8.04 us  [next_chip(): lax.ppermute(value, DP, tuple((((i + 2 - 4 * (i % 2)) % 8, i) for i in ra...]
  transfers between devices with their start and end apart: 10 -> 12, of which waited for: 6 -> 7; matrix products, arithmetic and copies ran while one was open for 2% -> 2% of each run, Pallas kernels for 9% -> 0%
where the time goes in v4:
time: 218 us; the launch traced here: 217 us
  waiting for transfers between devices  113 us (52%)
  Pallas kernels  52.4 us (24%)
  starting transfers between devices  32.1 us (15%)
  between operations  14.3 us (7%)
  local copies, waits for them, and re-layouts  3.62 us (2%)
  other arithmetic  2.51 us (1%)
    ppermute x3, waiting for transfers between devices, next_chip(): lax.ppermute(value, DP, tuple((((i + 2 - 4 * (i % 2)) % 8, i) for i in ra...  42 us
    all_to_all x1, waiting for transfers between devices, body(): lax.all_to_all(partial.reshape(tp_count, pairs, half), TP, split_axis=0,...  37 us
    pallas_call x1, Pallas kernels, head(): pl.pallas_call(functools.partial(head_kernel, steps, rows // 4, k_blocks,...  26.3 us
    all_to_all x1, waiting for transfers between devices, body(): lax.all_to_all(sent, ('z', 'y', 'xh'), split_axis=0, concat_axis=0, tiled...  25.6 us
    pallas_call x1, Pallas kernels, attention(): pl.pallas_call(attention_kernel, grid_spec=pltpu.PrefetchScalarGridSpec(n...  19.1 us
    all_to_all x1, starting transfers between devices, body(): lax.all_to_all(sent, ('z', 'y', 'xh'), split_axis=0, concat_axis=0, tiled...  8.1 us
    all_to_all x1, starting transfers between devices, body(): lax.all_to_all(partial.reshape(tp_count, pairs, half), TP, split_axis=0,...  8.09 us
    ppermute x3, starting transfers between devices, next_chip(): lax.ppermute(value, DP, tuple((((i + 2 - 4 * (i % 2)) % 8, i) for i in ra...  8.04 us
  transfers between devices with their start and end apart: 12, of which 7 were waited for; matrix products, arithmetic and copies ran while one was open for 2% of the time, Pallas kernels for 0%

profile of v4, /device:TPU:0, one launch (start us, length us, event | category | flops | bytes accessed | tf_op | source)
XLA Modules:
  0.0 217.5 jit_solution(13778476595406280723)
XLA Ops:
  7.2 0.0 copy-start
  7.2 19.1 %latent_attention.1 = (bf16[2,192,3584]{2,1,0:T(8,128)(2,1)}, bf16[3584,512]{1,0:T(8,128)(2,1)}, bf16[3584,512]{1,0:T(8,128)(2,1)}) custom-call(s32[64]{0:T(128)} %lengths_ref.1, bf16[64,3,4,576]{3,2,1,0:T(4,128)(2,1)} %queries_ref.1, bf16[64,576,128]{2,1,0:T(8,128)(2,1)} %bitcast.63, bf16[3,64,576]{2,1,0:T(8,128)(2,1)} %bitcast.68, ...), custom_call_target="tpu_custom_call" | custom-call | flops 1711276032 | bytes 16777216 | tf_op jit(solution)/shard_map/latent_attention/pallas_call | solution.py:160
  26.3 0.0 copy-start.3
  26.3 2.9 %collective-permute-start = (bf16[3584,512]{1,0:T(8,128)(2,1)}, bf16[3584,512]{1,0:T(8,128)(2,1)}, u32[]{:S(2)}, u32[]{:S(2)}) collective-permute-start(bf16[3584,512]{1,0:T(8,128)(2,1)} %get-tuple-element.9), channel_id=1, source_target_pairs={{32,0},{112,16},{64,32},{16,48},{96,64},{48,80},{0,96},{80,112},{3... | collective-permute-start | bytes 11010056 | tf_op jit(solution)/shard_map/ppermute | solution.py:478
  29.2 8.1 %all-to-all-start = ((bf16[16,24,3584]{2,1,0:T(8,128)(2,1)}), bf16[16,24,3584]{2,1,0:T(8,128)(2,1)}, u32[]{:S(2)}, u32[]{:S(2)}) async-start(bf16[16,24,3584]{2,1,0:T(8,128)(2,1)} %bitcast.64), calls=%async_computation | async-start | bytes 5505024 | tf_op jit(solution)/shard_map/all_to_all | solution.py:510
  37.3 0.0 all-gather.2.cloned.1.call-start
  37.4 0.1 dynamic_slice.22
  37.5 37.0 %all-to-all-done.parts_ref = bf16[16,24,3584]{2,1,0:T(8,128)(2,1)} async-done(((bf16[16,24,3584]{2,1,0:T(8,128)(2,1)}), bf16[16,24,3584]{2,1,0:T(8,128)(2,1)}, u32[]{:S(2)}, u32[]{:S(2)}) %all-to-all-start) | async-done | bytes 2752544 | tf_op jit(solution)/shard_map/all_to_all | solution.py:510
  74.5 2.2 sum_residual_gain.1
  76.7 6.4 %collective-permute-start.1 = (bf16[24,3584]{1,0:T(8,128)(2,1)S(1)}, bf16[24,3584]{1,0:T(8,128)(2,1)S(1)}, u32[]{:S(2)}, u32[]{:S(2)}) collective-permute-start(bf16[24,3584]{1,0:T(8,128)(2,1)S(1)} %sum_residual_gain.1), channel_id=1, source_target_pairs={{0,64},{64,0},{1,65},{65,1},{2,66},{66,2},{3,67},{67,3},{4,68},{68... | collective-permute-start | bytes 516104 | tf_op jit(solution)/shard_map/ppermute | solution.py:515
  83.1 3.7 %collective-permute-done.1 = bf16[24,3584]{1,0:T(8,128)(2,1)S(1)} collective-permute-done((bf16[24,3584]{1,0:T(8,128)(2,1)S(1)}, bf16[24,3584]{1,0:T(8,128)(2,1)S(1)}, u32[]{:S(2)}, u32[]{:S(2)}) %collective-permute-start.1) | collective-permute-done | bytes 172064 | tf_op jit(solution)/shard_map/ppermute | solution.py:515
  86.8 0.8 maximum_select_fusion
  87.5 0.0 all-gather.2.cloned.1.call-update
  87.6 0.1 collective-permute-start.2
  87.7 0.8 maximum_select_fusion.1.after_ref
  88.4 2.4 %collective-permute-start.3 = (bf16[3584,512]{1,0:T(8,128)(2,1)}, bf16[3584,512]{1,0:T(8,128)(2,1)}, u32[]{:S(2)}, u32[]{:S(2)}) collective-permute-start(bf16[3584,512]{1,0:T(8,128)(2,1)} %value_after.1), channel_id=1, source_target_pairs={{32,0},{112,16},{64,32},{16,48},{96,64},{48,80},{0,96},{80,112},{3... | collective-permute-start | bytes 11010056 | tf_op jit(solution)/shard_map/ppermute | solution.py:478
  90.8 0.8 collective-permute-start.4
  91.6 41.0 %collective-permute-done.3.refs_3_ = bf16[3584,512]{1,0:T(8,128)(2,1)} collective-permute-done((bf16[3584,512]{1,0:T(8,128)(2,1)}, bf16[3584,512]{1,0:T(8,128)(2,1)}, u32[]{:S(2)}, u32[]{:S(2)}) %collective-permute-start.3) | collective-permute-done | bytes 3670048 | tf_op jit(solution)/shard_map/ppermute | solution.py:478
  132.6 0.0 collective-permute-start.5
  132.6 2.7 %collective-permute-start.7 = (s32[512,3]{0,1:T(4,128)S(1)}, s32[512,3]{0,1:T(4,128)S(1)}, u32[]{:S(2)}, u32[]{:S(2)}) collective-permute-start(s32[512,3]{0,1:T(4,128)S(1)} %bitcast.76), channel_id=1, source_target_pairs={{32,0},{112,16},{64,32},{16,48},{96,64},{48,80},{0,96},{80,112},{3... | collective-permute-start | bytes 18440 | tf_op jit(solution)/shard_map/ppermute | solution.py:478
  135.3 0.1 add_multiply_fusion
  135.4 0.1 reshape_reshape.3
  135.6 0.1 reshape.254
  135.7 1.0 collective-permute-done.7
  136.7 0.5 collective-permute-start.8
  137.2 0.1 reshape.250
  137.3 1.7 collective-permute-done.6
  139.0 0.1 reshape.248
  139.2 0.1 stack_reshape.13
  139.3 0.1 stack_reshape.12
  139.4 0.1 stack_reshape.14
  139.5 0.0 collective-permute-done.8
  139.5 0.1 reshape.252
  139.7 0.1 sub.30
  139.8 0.1 stack_reshape.15
  139.9 0.1 broadcast_subtract_fusion
  140.0 1.7 copy.32.refs_6_
  141.7 0.0 collective-permute-done.2.refs_1_
  141.7 0.0 collective-permute-done.4.refs_4_
  141.7 2.7 %all-gather.2.cloned.1.call-done = bf16[16,2,24,3584]{3,2,1,0:T(8,128)(2,1)} async-done(((bf16[1,2,24,3584]{3,2,1,0:T(8,128)(2,1)}), bf16[16,2,24,3584]{3,2,1,0:T(8,128)(2,1)}) %all-gather.2.cloned.1.call-update) | async-done | bytes 5505040 | tf_op jit(solution)/shard_map/all_gather | solution.py:519
  144.3 26.3 %logits_and_shard_softmax.1 = bf16[256,3200]{1,0:T(8,128)(2,1)} custom-call(bf16[2,384,3584]{2,1,0:T(8,128)(2,1)} %bitcast.79, bf16[7168,512]{1,0:T(8,128)(2,1)} %refs_0_.1, bf16[7168,512]{1,0:T(8,128)(2,1)} %collective-permute-done.2.refs_1_, bf16[3584,512]{1,0:T(8,128)(2,1)} %collective-permute-done.after_ref.refs_2_, ...), custom_call_target="tpu_custom_call" | custom-call | flops 11274289152 | bytes 34865152 | tf_op jit(solution)/shard_map/logits_and_shard_softmax/pallas_call | solution.py:327
  170.7 8.1 %all-to-all-start.1 = ((bf16[32,8,3200]{2,1,0:T(8,128)(2,1)}), bf16[32,8,3200]{2,1,0:T(8,128)(2,1)}, u32[]{:S(2)}, u32[]{:S(2)}) async-start(bf16[32,8,3200]{2,1,0:T(8,128)(2,1)} %bitcast.65), calls=%async_computation.1 | async-start | bytes 3276800 | tf_op jit(solution)/shard_map/all_to_all | solution.py:522
  178.8 0.1 pad_add_fusion.place_ref
  178.9 25.6 %all-to-all-done.1.got_ref = bf16[32,8,3200]{2,1,0:T(8,128)(2,1)} async-done(((bf16[32,8,3200]{2,1,0:T(8,128)(2,1)}), bf16[32,8,3200]{2,1,0:T(8,128)(2,1)}, u32[]{:S(2)}, u32[]{:S(2)}) %all-to-all-start.1) | async-done | bytes 1638432 | tf_op jit(solution)/shard_map/all_to_all | solution.py:522
  204.4 4.8 %owned_log_probs.1 = (f32[3,4,65536]{2,1,0:T(4,128)}, f32[3,8,128]{2,1,0:T(8,128)S(1)}) custom-call(s32[2]{0:T(128)S(1)} %pad_add_fusion.place_ref, bf16[32,8,3200]{2,1,0:T(8,128)(2,1)} %all-to-all-done.1.got_ref), custom_call_target="tpu_custom_call" | custom-call | flops 3145728 | bytes 4718592 | tf_op jit(solution)/shard_map/owned_log_probs/pallas_call | solution.py:427
  209.2 0.2 slice_reduce_fusion
  209.4 0.5 broadcast_multiply_fusion
  209.9 0.7 copy.33
  (25 shorter events, 0.2 us)
Async XLA Ops:
  7.2 30.3 %copy-start = (bf16[64,3,7168]{2,0,1:T(8,128)(2,1)S(1)}, bf16[64,3,7168]{2,0,1:T(8,128)(2,1)}, u32[]{:S(2)}) copy-start(bf16[64,3,7168]{2,0,1:T(8,128)(2,1)} %param.17) | copy-start | bytes 8257540
  26.3 11.1 %copy-start.3 = (f32[7168]{0:T(1024)S(1)}, f32[7168]{0:T(1024)}, u32[]{:S(2)}) copy-start(f32[7168]{0:T(1024)} %param.18) | copy-start | bytes 86020
  26.3 48.2 %collective-permute-start = (bf16[3584,512]{1,0:T(8,128)(2,1)}, bf16[3584,512]{1,0:T(8,128)(2,1)}, u32[]{:S(2)}, u32[]{:S(2)}) collective-permute-start(bf16[3584,512]{1,0:T(8,128)(2,1)} %get-tuple-element.9), channel_id=1, source_target_pairs={{32,0},{112,16},{64,32},{16,48},{96,64},{48,80},{0,96},{80,112},{3... | collective-permute-start | bytes 11010056 | tf_op jit(solution)/shard_map/ppermute | solution.py:478
  29.2 45.3 %all-to-all-start = ((bf16[16,24,3584]{2,1,0:T(8,128)(2,1)}), bf16[16,24,3584]{2,1,0:T(8,128)(2,1)}, u32[]{:S(2)}, u32[]{:S(2)}) async-start(bf16[16,24,3584]{2,1,0:T(8,128)(2,1)} %bitcast.64), calls=%async_computation | async-start | bytes 5505024 | tf_op jit(solution)/shard_map/all_to_all | solution.py:510
  37.3 107.0 %all-gather.2.cloned.1.call-start = ((), (), s32[]{:S(2)}) async-start(), calls=%async_computation.2 | async-start | bytes 5849088 | tf_op jit(solution)/shard_map/all_gather | solution.py:519
  76.7 10.1 %collective-permute-start.1 = (bf16[24,3584]{1,0:T(8,128)(2,1)S(1)}, bf16[24,3584]{1,0:T(8,128)(2,1)S(1)}, u32[]{:S(2)}, u32[]{:S(2)}) collective-permute-start(bf16[24,3584]{1,0:T(8,128)(2,1)S(1)} %sum_residual_gain.1), channel_id=1, source_target_pairs={{0,64},{64,0},{1,65},{65,1},{2,66},{66,2},{3,67},{67,3},{4,68},{68... | collective-permute-start | bytes 516104 | tf_op jit(solution)/shard_map/ppermute | solution.py:515
  87.6 54.1 %collective-permute-start.2 = (bf16[7168,512]{1,0:T(8,128)(2,1)}, bf16[7168,512]{1,0:T(8,128)(2,1)}, u32[]{:S(2)}, u32[]{:S(2)}) collective-permute-start(bf16[7168,512]{1,0:T(8,128)(2,1)} %refs_0_.1), channel_id=1, source_target_pairs={{0,16},{16,0},{1,17},{17,1},{2,18},{18,2},{3,19},{19,3},{4,20},{20... | collective-permute-start | bytes 22020104 | tf_op jit(solution)/shard_map/ppermute | solution.py:475
  88.4 44.1 %copy-start.2 = (s32[512,3,1]{0,2,1:T(1,128)S(1)}, s32[512,3,1]{0,2,1:T(1,128)}, u32[]{:S(2)}) copy-start(s32[512,3,1]{0,2,1:T(1,128)} %param.20) | copy-start | bytes 18436
  88.4 47.1 %copy-start.4 = (s32[512,3]{0,1:T(4,128)S(1)}, s32[512,3]{0,1:T(4,128)}, u32[]{:S(2)}) copy-start(s32[512,3]{0,1:T(4,128)} %param.21) | copy-start | bytes 18436
  88.4 44.1 %collective-permute-start.3 = (bf16[3584,512]{1,0:T(8,128)(2,1)}, bf16[3584,512]{1,0:T(8,128)(2,1)}, u32[]{:S(2)}, u32[]{:S(2)}) collective-permute-start(bf16[3584,512]{1,0:T(8,128)(2,1)} %value_after.1), channel_id=1, source_target_pairs={{32,0},{112,16},{64,32},{16,48},{96,64},{48,80},{0,96},{80,112},{3... | collective-permute-start | bytes 11010056 | tf_op jit(solution)/shard_map/ppermute | solution.py:478
  90.8 50.8 %collective-permute-start.4 = (bf16[3584,512]{1,0:T(8,128)(2,1)}, bf16[3584,512]{1,0:T(8,128)(2,1)}, u32[]{:S(2)}, u32[]{:S(2)}) collective-permute-start(bf16[3584,512]{1,0:T(8,128)(2,1)} %collective-permute-done.after_ref.refs_2_), channel_id=1, source_target_pairs={{0,16},{16,0},{1,17},{17,1},{2,18},{18,2},{3,19},{19,3},{4,20},{20... | collective-permute-start | bytes 11010056 | tf_op jit(solution)/shard_map/ppermute | solution.py:475
  132.6 9.1 %collective-permute-start.5 = (bf16[3584,512]{1,0:T(8,128)(2,1)}, bf16[3584,512]{1,0:T(8,128)(2,1)}, u32[]{:S(2)}, u32[]{:S(2)}) collective-permute-start(bf16[3584,512]{1,0:T(8,128)(2,1)} %collective-permute-done.3.refs_3_), channel_id=1, source_target_pairs={{0,16},{16,0},{1,17},{17,1},{2,18},{18,2},{3,19},{19,3},{4,20},{20... | collective-permute-start | bytes 11010056 | tf_op jit(solution)/shard_map/ppermute | solution.py:475
  132.6 4.1 %collective-permute-start.7 = (s32[512,3]{0,1:T(4,128)S(1)}, s32[512,3]{0,1:T(4,128)S(1)}, u32[]{:S(2)}, u32[]{:S(2)}) collective-permute-start(s32[512,3]{0,1:T(4,128)S(1)} %bitcast.76), channel_id=1, source_target_pairs={{32,0},{112,16},{64,32},{16,48},{96,64},{48,80},{0,96},{80,112},{3... | collective-permute-start | bytes 18440 | tf_op jit(solution)/shard_map/ppermute | solution.py:478
  135.3 3.7 %collective-permute-start.6 = (s32[512,3]{0,1:T(4,128)S(1)}, s32[512,3]{0,1:T(4,128)S(1)}, u32[]{:S(2)}, u32[]{:S(2)}) collective-permute-start(s32[512,3]{0,1:T(4,128)S(1)} %bitcast.77), channel_id=1, source_target_pairs={{0,16},{16,0},{1,17},{17,1},{2,18},{18,2},{3,19},{19,3},{4,20},{20... | collective-permute-start | bytes 18440 | tf_op jit(solution)/shard_map/ppermute | solution.py:475
  136.7 2.8 %collective-permute-start.8 = (s32[512,3]{0,1:T(4,128)S(1)}, s32[512,3]{0,1:T(4,128)S(1)}, u32[]{:S(2)}, u32[]{:S(2)}) collective-permute-start(s32[512,3]{0,1:T(4,128)S(1)} %collective-permute-done.7), channel_id=1, source_target_pairs={{0,16},{16,0},{1,17},{17,1},{2,18},{18,2},{3,19},{19,3},{4,20},{20... | collective-permute-start | bytes 18440 | tf_op jit(solution)/shard_map/ppermute | solution.py:475
  144.3 66.3 %copy-start.1 = (bf16[64,3,7168]{2,0,1:T(8,128)(2,1)S(1)}, bf16[64,3,7168]{2,0,1:T(8,128)(2,1)}, u32[]{:S(2)}) copy-start(bf16[64,3,7168]{2,0,1:T(8,128)(2,1)} %param.17) | copy-start | bytes 8257540
  170.7 33.8 %all-to-all-start.1 = ((bf16[32,8,3200]{2,1,0:T(8,128)(2,1)}), bf16[32,8,3200]{2,1,0:T(8,128)(2,1)}, u32[]{:S(2)}, u32[]{:S(2)}) async-start(bf16[32,8,3200]{2,1,0:T(8,128)(2,1)} %bitcast.65), calls=%async_computation.1 | async-start | bytes 3276800 | tf_op jit(solution)/shard_map/all_to_all | solution.py:522
Sparse Core Ops, SparseCore 0:
  87.7 56.6 all-gather.1
